TPU v7x, 32 devices: a whole 2x2x4 slice. The times are simulated.
32 devices in a mesh: grid: 8 (over z, core), occ: 4 (over y, x).
Axes of the slice: x: 2, y: 2, z: 4, core: 2. Of those that a mesh axis runs over, the one named last changes fastest.
Arguments:
- orbital_values: bfloat16 [2048, 16000], P('grid', 'occ'), may hold values from -6 to 6
- occupied: bfloat16 [16000, 512], P('occ', 'grid'), may hold values from -0.046875 to 0.046875
- trial: bfloat16 [16000, 512], P('occ', 'grid'), may hold values from -0.046875 to 0.046875
- point_weights: float32 [2048], P('grid'), may hold values from 0.1 to 1
- batch_sizes: int32 [64], P('grid'), may hold values from 1 to 32, 1024 in all
- significant: int32 [64, 128], P('grid', 'occ'), may hold values 0 or 1
Outputs:
- exchange: float32 [16000, 512], P('occ', 'grid')
Inputs may be any that keep to these rules, and one draw needn't show every extreme that they name: `batch_sizes`: batch sizes sum to 1024 and the largest is exactly 32.
All inputs are finite; a program needn't handle non-finite values. No bound on the sum of `batch_sizes` or of `significant` on one device may be relied on, other than what follows from the above.
Results may differ from a plain program's by a relative error of at most 0.0027.
Values may be sent and summed in bfloat16 or wider, within the bound.
No kernel may reach another device: no remote copies, remote signals or barrier semaphores. Data moves between devices by JAX's collectives and lax.ppermute only.
A program may use at most 64 MiB of HBM per device.

v0:
```python
import math

import jax
import jax.numpy as jnp
from jax import lax
from jax.experimental import pallas as pl
from jax.experimental.pallas import tpu as pltpu
from jax.sharding import PartitionSpec as P

BF16, F32 = jnp.bfloat16, jnp.float32
VMEM_LIMIT = 48 * 1024 * 1024
WHOLE = pl.BlockSpec(memory_space=pltpu.VMEM)
SCALARS = pl.BlockSpec(memory_space=pltpu.SMEM)


def screen(values, sizes, significant):
    rows, cols = values.shape
    batches = sizes.shape[0]
    blocks = significant.shape[1]
    blocked = (
        values.reshape(batches, rows // batches, blocks, cols // blocks)
        * significant.astype(values.dtype)[:, None, :, None]
    )
    position = lax.broadcasted_iota(jnp.int32, (batches, rows // batches), 1)
    live = (position < sizes[:, None]).astype(jnp.float32).reshape(rows)
    return (blocked.reshape(rows, cols), live)


def any_sizes(orbital_values, occupied, trial, point_weights, batch_sizes, significant):
    screened, live = screen(orbital_values, batch_sizes, significant)
    rows, cols = screened.shape
    grid_count, occ_count = lax.axis_size("grid"), lax.axis_size("occ")
    columns = occupied.shape[1]
    me = lax.axis_index("grid")
    ring = [(i, (i + 1) % grid_count) for i in range(grid_count)]
    occ_ring = [(i, (i + 1) % occ_count) for i in range(occ_count)]

    def project_one(step, carry):
        panel, terms = carry
        term = jnp.dot(screened, panel, preferred_element_type=F32)
        terms = lax.dynamic_update_index_in_dim(terms, term, (me - step) % grid_count, 0)
        return lax.ppermute(panel, "grid", ring), terms

    joined = jnp.concatenate((occupied, trial), axis=1)
    terms = jnp.zeros((grid_count, rows, 2 * columns), F32)
    terms = lax.fori_loop(0, grid_count, project_one, (joined, terms))[1]

    def add_one(step, carry):
        moving, held = carry
        moving = lax.ppermute(moving, "occ", occ_ring)
        return moving, held + moving

    terms = lax.fori_loop(0, occ_count - 1, add_one, (terms, terms))[1]
    orbitals, response = terms[:, :, :columns], terms[:, :, columns:]
    density = jnp.sum(orbitals * response, axis=(0, 2)) * (1.0 / math.sqrt(columns * grid_count))
    weight = (point_weights * live)[None, :, None]
    kernel = (weight * (density[None, :, None] * orbitals + response)).astype(BF16)

    def contract_one(step, held):
        owner = (me + grid_count - 1 - step) % grid_count
        part = lax.dynamic_index_in_dim(kernel, owner, 0, keepdims=False)
        term = lax.dot_general(
            part, screened, (((0,), (0,)), ((), ())), preferred_element_type=F32
        )
        return lax.ppermute(held, "grid", ring) + term

    return lax.fori_loop(0, grid_count, contract_one, jnp.zeros((columns, cols), F32))


def compact(mine, got, mine_sig, got_sig, mine_to, got_to, width, tile, first):
    half, rows = mine.shape
    blocks = mine_sig.shape[0]
    per_window = rows // tile

    def body(first_ref, mine_ref, got_ref, msig_ref, gsig_ref, mto_ref, gto_ref, *outs):
        block_of = lax.broadcasted_iota(jnp.int32, (half, blocks), 0)
        begin = lax.broadcasted_iota(jnp.int32, (half, blocks), 1) * width
        spread = ((block_of >= begin) & (block_of < begin + width)).astype(F32).astype(BF16)
        slot = lax.broadcasted_iota(jnp.int32, (rows, 2 * rows), 1)

        def part(value_ref, sig_ref, to_ref):
            kept = jnp.dot(spread, sig_ref[...], preferred_element_type=F32)
            screened = (value_ref[...].astype(F32) * kept).astype(BF16)
            place = (to_ref[...] == slot).astype(F32).astype(BF16)
            return jnp.dot(screened, place, preferred_element_type=F32)

        window = part(mine_ref, msig_ref, mto_ref) + part(got_ref, gsig_ref, gto_ref)
        for j in range(2 * per_window):
            outs[j][...] = window[:, j * tile : (j + 1) * tile].astype(BF16)
        outs[-1][...] = jnp.where(
            first_ref[0] == 0, window[:, rows - tile : rows], window[:, rows : rows + tile]
        ).astype(BF16)

    shape = jax.ShapeDtypeStruct((half, tile), BF16)
    return pl.pallas_call(
        body,
        out_shape=(shape,) * (2 * per_window + 1),
        in_specs=[SCALARS] + [WHOLE] * 6,
        out_specs=(WHOLE,) * (2 * per_window + 1),
        compiler_params=pltpu.CompilerParams(vmem_limit_bytes=VMEM_LIMIT),
        name="compact",
        cost_estimate=pl.CostEstimate(
            flops=8 * half * rows * rows, bytes_accessed=8 * half * rows, transcendentals=0
        ),
    )(first[None], mine, got, mine_sig, got_sig, mine_to, got_to)


def read_tiles(tiles, refs):
    q, values = 0, []
    for parts in tiles:
        value = refs[q][...]
        for ref in refs[q + 1 : q + len(parts)]:
            value = value + ref[...]
        q += len(parts)
        values.append(value)
    return values


def project(panels, tiles, tile, shares, core):
    both, half = panels[0].shape
    piece = tile // shares
    count, number = len(tiles), len(panels)

    def body(core_ref, *refs):
        panel_refs, tile_refs = refs[:number], refs[number:-3]
        keep_ref, give_ref, terms_ref = refs[-3:]
        values = read_tiles(tiles, tile_refs)
        stacked = jnp.concatenate([ref[...] for ref in panel_refs])
        for s in range(0, count, 2):
            pair = jnp.concatenate(values[s : s + 2], axis=1)
            terms = jnp.dot(stacked, pair, preferred_element_type=F32)
            for p in range(number):
                turned = terms[p * both : (p + 1) * both].T
                for j in range(len(values[s : s + 2])):
                    q = p * count + s + j
                    terms_ref[q] = turned[j * tile : (j + 1) * tile].reshape(
                        2, shares // 2, piece, both
                    )
                    keep_ref[q] = terms_ref[q, core_ref[0]]
                    give_ref[q] = terms_ref[q, 1 - core_ref[0]]

    shape = jax.ShapeDtypeStruct((number * count, shares // 2, piece, both), F32)
    return pl.pallas_call(
        body,
        out_shape=(shape, shape),
        in_specs=[SCALARS] + [WHOLE] * (number + sum(map(len, tiles))),
        out_specs=(WHOLE, WHOLE),
        scratch_shapes=[pltpu.VMEM((number * count, 2, shares // 2, piece, both), F32)],
        compiler_params=pltpu.CompilerParams(vmem_limit_bytes=VMEM_LIMIT),
        name="project",
        cost_estimate=pl.CostEstimate(
            flops=2 * number * both * half * count * tile,
            bytes_accessed=2 * half * (number * both + count * tile)
            + 4 * number * count * tile * both,
            transcendentals=0,
        ),
    )(core[None], *panels, *sum(tiles, ()))


def contract(kernel, tiles, core):
    points, columns = kernel.shape
    half, tile = tiles[0][0].shape
    own = columns // 2
    count = len(tiles)

    def body(core_ref, kernel_ref, *refs):
        tile_refs, mine_ref, other_ref = refs[:-2], refs[-2], refs[-1]
        values = read_tiles(tiles, tile_refs)
        first = core_ref[0] == 0
        total = None
        for s in range(0, count, 2):
            pair = jnp.concatenate(values[s : s + 2], axis=1)
            turned = kernel_ref[s * tile : s * tile + pair.shape[1]].astype(F32).T
            low, high = turned[:own], turned[own:]
            turned = jnp.concatenate(
                (jnp.where(first, low, high), jnp.where(first, high, low))
            ).astype(BF16)
            term = lax.dot_general(
                turned, pair, (((1,), (1,)), ((), ())), preferred_element_type=F32
            )
            total = term if total is None else total + term
        mine_ref[...] = total[:own]
        other_ref[...] = total[own:]

    shape = jax.ShapeDtypeStruct((own, half), F32)
    return pl.pallas_call(
        body,
        out_shape=(shape, shape),
        in_specs=[SCALARS] + [WHOLE] * (1 + sum(map(len, tiles))),
        out_specs=(WHOLE, WHOLE),
        compiler_params=pltpu.CompilerParams(vmem_limit_bytes=VMEM_LIMIT),
        name="contract",
        cost_estimate=pl.CostEstimate(
            flops=2 * columns * half * points,
            bytes_accessed=2 * points * half + 4 * columns * half,
            transcendentals=0,
        ),
    )(core[None], kernel, *sum(tiles, ()))


def finish(core, ours, back, scale):
    own, half = ours.shape

    def body(core_ref, ours_ref, back_ref, out_ref):
        first = core_ref[0] == 0
        out_ref[:, :half] = jnp.where(first, ours_ref[...], back_ref[...]) * scale
        out_ref[:, half:] = jnp.where(first, back_ref[...], ours_ref[...]) * scale

    return pl.pallas_call(
        body,
        out_shape=jax.ShapeDtypeStruct((own, 2 * half), F32),
        in_specs=[SCALARS, WHOLE, WHOLE],
        out_specs=WHOLE,
        compiler_params=pltpu.CompilerParams(vmem_limit_bytes=VMEM_LIMIT),
        name="finish",
    )(core[None], ours, back)


def per_device(orbital_values, occupied, trial, point_weights, batch_sizes, significant):
    rows, cols = orbital_values.shape
    batches = batch_sizes.shape[0]
    slots = rows // batches
    blocks = significant.shape[1]
    columns = occupied.shape[1]
    grid_count = lax.axis_size("grid")
    occ_count = lax.axis_size("occ")
    chips = grid_count // 2
    shares = 2 * occ_count
    half = cols // 2
    total = columns * grid_count
    place = lax.axis_index("grid")
    chip, core = place // 2, place % 2
    occ = lax.axis_index("occ")
    member = core * occ_count + occ

    def flip(x, axis, bit):
        count = lax.axis_size(axis)
        return lax.ppermute(x, axis, [(i, i ^ bit) for i in range(count)])

    def along(pairs):
        return [(2 * a + c, 2 * b + c) for a, b in pairs for c in range(2)]

    def doubled(x, axis, bit, dim):
        got = flip(x, axis, bit)
        mine = (lax.axis_index(axis) & bit) == 0
        return jnp.where(
            mine, jnp.concatenate((x, got), axis=dim), jnp.concatenate((got, x), axis=dim)
        )

    def halves(whole, axis):
        size = whole.shape[axis] // 2
        mine = lax.dynamic_slice_in_dim(whole, core * size, size, axis)
        return mine, lax.dynamic_slice_in_dim(whole, (1 - core) * size, size, axis)

    grid_bits = [1 << b for b in range(grid_count.bit_length() - 1)]
    occ_bits = [1 << b for b in range(occ_count.bit_length() - 1)]

    mine, other = halves(orbital_values.T, 0)
    got = flip(other, "grid", 1)
    mine_sig, other_sig = halves(significant.T, 0)
    got_sig = flip(other_sig, "grid", 1)

    told = jnp.concatenate((batch_sizes.astype(F32), point_weights))[None]
    for bit in grid_bits:
        told = doubled(told, "grid", bit, 0)
    sizes = told[:, :batches].astype(jnp.int32).reshape(-1)
    weights = told[:, batches:].reshape(-1)

    batch = lax.broadcasted_iota(jnp.int32, (sizes.shape[0], sizes.shape[0]), 0)
    before = lax.broadcasted_iota(jnp.int32, (sizes.shape[0], sizes.shape[0]), 1) < batch
    start = jnp.sum(jnp.where(before, sizes[None, :], 0), axis=1)
    position = lax.broadcasted_iota(jnp.int32, (sizes.shape[0], slots), 1)
    to = jnp.where(position < sizes[:, None], start[:, None] + position, -4 * rows * grid_count)
    to = to.reshape(grid_count, rows)
    first = start.reshape(chips, -1)[:, 0]
    margin = rows // 2
    nominal = rows * lax.iota(jnp.int32, chips)
    fits = jnp.all(jnp.abs(first - nominal) <= margin) & (jnp.sum(sizes) <= rows * chips)

    tile = margin if margin % (8 * shares) == 0 else rows
    base = rows * chip - margin
    mine_to = lax.dynamic_index_in_dim(to, place, 0, keepdims=False) - base
    got_to = lax.dynamic_index_in_dim(to, place ^ 1, 0, keepdims=False) - base
    *own_tiles, edge = compact(
        mine,
        got,
        jnp.repeat(mine_sig.astype(BF16), slots, axis=1),
        jnp.repeat(got_sig.astype(BF16), slots, axis=1),
        mine_to[:, None],
        got_to[:, None],
        cols // blocks,
        tile,
        chip,
    )

    mine_panel, other_panel = halves(jnp.concatenate((occupied, trial), axis=1).T, 1)
    got_panel = flip(other_panel, "grid", 1)
    panels = jnp.where(
        core == 0,
        jnp.concatenate(
            (mine_panel[:columns], got_panel[:columns], mine_panel[columns:], got_panel[columns:])
        ),
        jnp.concatenate(
            (got_panel[:columns], mine_panel[:columns], got_panel[columns:], mine_panel[columns:])
        ),
    )

    piece = tile // shares
    per_window = rows // tile
    tile_count = (chips + 1) * per_window
    tile_iota = lax.iota(jnp.int32, tile_count)
    last = chips - 1
    ends = [(0, 1), (last, last - 1)]
    homes = [(b, a) for a, b in ends]
    none = -2 * per_window
    low, high = own_tiles[:per_window], own_tiles[per_window:]

    def sent(tiles, pairs):
        return [lax.ppermute(x, "grid", along(pairs)) for x in tiles]

    stages = []
    leftward, rightward = low, high
    far_panels = None
    for t in range(1, last):
        to_left = [(a, a - 1) for a in range(1, chips) if t == 1 or a + t - 1 < chips]
        to_right = [(a, a + 1) for a in range(last) if t == 1 or a + 2 - t > 0]
        from_right, from_left = [], []
        for x, y in zip(leftward, rightward):
            from_right += sent([x], to_left)
            from_left += sent([y], to_right)
        (edge,) = sent([edge], [(t - 1, t), (chips - t, last - t)])
        if t == 1:
            from_right = [x + y for x, y in zip(from_right, high)]
            from_left = [x + y for x, y in zip(from_left, low)]
            (far_panels,) = sent([panels], ends)
        right = jnp.where((chip + t <= last) | (t == 1), (chip + t) * per_window, none)
        left = jnp.where((chip + 1 - t > 0) | (t == 1), (chip + 1 - t) * per_window, none)
        edge_at = jnp.where(
            chip == t, per_window - 1, jnp.where(chip == last - t, chips * per_window, none)
        )
        if 2 * t > last:
            at = jnp.maximum(right, left)
            jobs = [((x, y), at + j) for j, (x, y) in enumerate(zip(from_right, from_left))]
        else:
            jobs = [((x,), right + j) for j, x in enumerate(from_right)]
            jobs += [((x,), left + j) for j, x in enumerate(from_left)]
        stages.append(jobs + [((edge,), edge_at)])
        leftward, rightward = from_right, from_left
    late = [
        (x, y) for x, y in zip(sent(leftward, homes[:1]), sent(rightward, homes[1:]))
    ]

    def summed(panels, tiles):
        keep, give = project(panels, tiles, tile, shares, core)
        value = keep + flip(give, "grid", 1)
        for bit in reversed(occ_bits):
            upper = (occ & bit) != 0
            low_part, high_part = value[:, :bit], value[:, bit:]
            got = flip(jnp.where(upper, low_part, high_part), "occ", bit)
            value = jnp.where(upper, high_part, low_part) + got
        return value[:, 0]

    def shared_density(value, at):
        product = jnp.sum(value[:, :, : 2 * columns] * value[:, :, 2 * columns :], axis=2)
        here = (at[:, None] == tile_iota[None, :])[:, :, None]
        return jnp.sum(jnp.where(here, product[:, None], 0.0), axis=0)

    per_group = -(-len(stages) // 2)
    first_jobs = sum(stages[:per_group], [])
    second_jobs = sum(stages[per_group:], [])
    first_at = jnp.stack([at for _, at in first_jobs])
    second_at = jnp.stack([at for _, at in second_jobs])
    first_value = summed([panels], [w for w, _ in first_jobs])
    far_count = per_window + 1
    second_tiles, first_value = lax.optimization_barrier(
        ([w for w, _ in second_jobs], first_value)
    )
    value = summed([panels, far_panels], second_tiles)
    far_value = value[-far_count:]
    second_value = value[: len(second_jobs)]
    density = shared_density(first_value, first_at) + shared_density(
        jnp.concatenate((second_value, far_value)),
        jnp.concatenate((second_at, second_at[-far_count:])),
    )
    density, late = lax.optimization_barrier((density, late))
    for bit in grid_bits[1:]:
        density = density + flip(density, "grid", bit)
    density = density * (1.0 / math.sqrt(total))
    density, edge = lax.optimization_barrier((density, edge))
    late = late + [tuple(sent([edge], homes))]

    tiles = [w for w, _ in first_jobs] + second_tiles + late
    values = [first_value, second_value, *sent([far_value], homes)]
    outer = lax.iota(jnp.int32, per_window)
    places = [
        first_at,
        second_at,
        jnp.where(
            chip == 0,
            jnp.concatenate((outer + last * per_window, outer[:1] + chips * per_window)),
            jnp.concatenate((outer + per_window, outer[:1] + per_window - 1)),
        ),
    ]

    at = tile_iota[:, None] * tile - margin + member * piece + lax.iota(jnp.int32, piece)[None, :]
    weight = jnp.sum(
        jnp.where(to.reshape(1, -1) == at.reshape(-1, 1), weights[None, :], 0.0), axis=1
    ).reshape(tile_count, piece)

    values, places = jnp.concatenate(values, axis=0), jnp.concatenate(places)
    here = (places[:, None] == tile_iota[None, :])[:, :, None]
    density_here = jnp.sum(jnp.where(here, density[None], 0.0), axis=1)[:, :, None]
    weight_here = jnp.sum(jnp.where(here, weight[None], 0.0), axis=1)[:, :, None]
    orbitals, response = values[:, :, : 2 * columns], values[:, :, 2 * columns :]
    kernel = (weight_here * (density_here * orbitals + response)).astype(BF16)[:, None]
    for bit in occ_bits:
        kernel = doubled(kernel, "occ", bit, 1)
    kernel = doubled(kernel, "grid", 1, 1).reshape(-1, 2 * columns)

    ours, theirs = contract(kernel, tiles, core)
    back = flip(theirs, "grid", 1)
    scale = 1.0 / math.sqrt(rows * grid_count)
    exchange = lax.cond(
        fits,
        lambda core, ours, back, *given: finish(core, ours, back, scale),
        lambda core, ours, back, *given: any_sizes(*given) * scale,
        core,
        ours,
        back,
        orbital_values,
        occupied,
        trial,
        point_weights,
        batch_sizes,
        significant,
    )
    return exchange.T


def solution(mesh):
    placed = (
        P("grid", "occ"),
        P("occ", "grid"),
        P("occ", "grid"),
        P("grid"),
        P("grid"),
        P("grid", "occ"),
    )
    return jax.shard_map(
        per_device, mesh=mesh, in_specs=placed, out_specs=P("occ", "grid"), check_vma=False
    )
```

profile of v0, /device:TPU:0, one launch (start us, length us, event | category | flops | bytes accessed | tf_op | source)
XLA Modules:
  0.0 184.0 jit_solution(11935470919490846494)
XLA Ops:
  0.0 2.7 %dynamic-slice_bitcast_fusion = (bf16[2000,256]{1,0:T(8,128)(2,1)}, bf16[2000,256]{1,0:T(8,128)(2,1)S(1)}) fusion(bf16[256,4000]{0,1:T(8,128)(2,1)} %param.14, s32[]{:T(128)S(6)} %select_n.289, s32[]{:T(128)S(6)} %select_n.288), kind=kLoop, calls=%fused_computation.16 | loop fusion | bytes 4096008 | tf_op jit(solution)/shard_map/dynamic_slice | solution.py:253
  6.0 2.7 %collective-permute-start.4 = (f32[2,264]{1,0:T(2,128)S(1)}, f32[2,264]{1,0:T(2,128)S(1)}, u32[]{:S(2)}, u32[]{:S(2)}) collective-permute-start(f32[2,264]{1,0:T(2,128)S(1)} %maximum_select_fusion.6), channel_id=1, source_target_pairs={{0,8},{4,12},{8,0},{12,4},{16,24},{20,28},{24,16},{28,20},{1,9},{5... | collective-permute-start | bytes 6344 | tf_op jit(solution)/shard_map/ppermute | solution.py:238
  8.7 1.4 dynamic-slice_bitcast_fusion.3
  10.3 3.0 %collective-permute-start.5 = (f32[4,264]{1,0:T(4,128)S(1)}, f32[4,264]{1,0:T(4,128)S(1)}, u32[]{:S(2)}, u32[]{:S(2)}) collective-permute-start(f32[4,264]{1,0:T(4,128)S(1)} %maximum_select_fusion.5), channel_id=1, source_target_pairs={{0,16},{4,20},{8,24},{12,28},{16,0},{20,4},{24,8},{28,12},{1,17},{... | collective-permute-start | bytes 12680 | tf_op jit(solution)/shard_map/ppermute | solution.py:238
  13.4 1.8 fusion.16
  16.7 1.8 compact.1
  18.5 3.5 %collective-permute-start.14 = (bf16[2000,128]{1,0:T(8,128)(2,1)S(1)}, bf16[2000,128]{1,0:T(8,128)(2,1)S(1)}, u32[]{:S(2)}, u32[]{:S(2)}) collective-permute-start(bf16[2000,128]{1,0:T(8,128)(2,1)S(1)} %get-tuple-element.349), channel_id=1, source_target_pairs={{0,8},{4,12},{8,16},{12,20},{16,24},{20,28},{1,9},{5,13},{9,17},{1... | collective-permute-start | bytes 1536008 | tf_op jit(solution)/shard_map/ppermute | solution.py:319
  22.1 1.3 collective-permute-start.12
  23.4 4.6 %collective-permute-start.10 = (bf16[2000,128]{1,0:T(8,128)(2,1)S(1)}, bf16[2000,128]{1,0:T(8,128)(2,1)S(1)}, u32[]{:S(2)}, u32[]{:S(2)}) collective-permute-start(bf16[2000,128]{1,0:T(8,128)(2,1)S(1)} %get-tuple-element.347), channel_id=1, source_target_pairs={{0,8},{4,12},{8,16},{12,20},{16,24},{20,28},{1,9},{5,13},{9,17},{1... | collective-permute-start | bytes 1536008 | tf_op jit(solution)/shard_map/ppermute | solution.py:319
  27.9 1.3 collective-permute-start.8
  29.2 5.4 %collective-permute-start.16 = (bf16[2000,128]{1,0:T(8,128)(2,1)S(1)}, bf16[2000,128]{1,0:T(8,128)(2,1)}, u32[]{:S(2)}, u32[]{:S(2)}) collective-permute-start(bf16[2000,128]{1,0:T(8,128)(2,1)S(1)} %get-tuple-element.350), channel_id=1, source_target_pairs={{0,8},{4,12},{24,16},{28,20},{1,9},{5,13},{25,17},{29,21},{2,10},{... | collective-permute-start | bytes 1536008 | tf_op jit(solution)/shard_map/ppermute | solution.py:319
  35.0 3.5 %collective-permute-done.12 = bf16[2000,128]{1,0:T(8,128)(2,1)S(1)} collective-permute-done((bf16[2000,128]{1,0:T(8,128)(2,1)S(1)}, bf16[2000,128]{1,0:T(8,128)(2,1)S(1)}, u32[]{:S(2)}, u32[]{:S(2)}) %collective-permute-start.12) | collective-permute-done | bytes 512032 | tf_op jit(solution)/shard_map/ppermute | solution.py:319
  38.7 6.4 %collective-permute-done.10 = bf16[2000,128]{1,0:T(8,128)(2,1)S(1)} collective-permute-done((bf16[2000,128]{1,0:T(8,128)(2,1)S(1)}, bf16[2000,128]{1,0:T(8,128)(2,1)S(1)}, u32[]{:S(2)}, u32[]{:S(2)}) %collective-permute-start.10) | collective-permute-done | bytes 512032 | tf_op jit(solution)/shard_map/ppermute | solution.py:319
  45.2 2.0 %collective-permute-done.8 = bf16[2000,128]{1,0:T(8,128)(2,1)S(1)} collective-permute-done((bf16[2000,128]{1,0:T(8,128)(2,1)S(1)}, bf16[2000,128]{1,0:T(8,128)(2,1)S(1)}, u32[]{:S(2)}, u32[]{:S(2)}) %collective-permute-start.8) | collective-permute-done | bytes 512032 | tf_op jit(solution)/shard_map/ppermute | solution.py:319
  47.4 6.7 %collective-permute-done.16.refs_5_.refs_4_ = bf16[2000,128]{1,0:T(8,128)(2,1)} collective-permute-done((bf16[2000,128]{1,0:T(8,128)(2,1)S(1)}, bf16[2000,128]{1,0:T(8,128)(2,1)}, u32[]{:S(2)}, u32[]{:S(2)}) %collective-permute-start.16) | collective-permute-done | bytes 512032 | tf_op jit(solution)/shard_map/ppermute | solution.py:319
  54.1 2.9 %project.2 = (f32[5,4,16,256]{3,2,1,0:T(8,128)S(1)}, f32[5,4,16,256]{3,2,1,0:T(8,128)}) custom-call(s32[1]{0:T(128)} %bitcast.2.core_ref, bf16[256,2000]{1,0:T(8,128)(2,1)S(1)} %maximum_select_fusion.refs_0_, bf16[2000,128]{1,0:T(8,128)(2,1)S(1)} %add.312.refs_1_.refs_0_, bf16[2000,128]{1,0:T(8,128)(2,1)S(1)} %add.314.refs_2_.refs_1_, ...), custom_call_target="tpu_custom_call" | custom-call | flops 655360000 | bytes 4239360 | tf_op jit(solution)/shard_map/project/pallas_call | solution.py:143
  57.2 1.3 copy.38
  58.5 5.5 %collective-permute-start.22 = (bf16[256,2000]{0,1:T(8,128)(2,1)}, bf16[256,2000]{0,1:T(8,128)(2,1)}, u32[]{:S(2)}, u32[]{:S(2)}) collective-permute-start(bf16[256,2000]{0,1:T(8,128)(2,1)} %copy.38), channel_id=1, source_target_pairs={{0,8},{4,12},{24,16},{28,20},{1,9},{5,13},{25,17},{29,21},{2,10},{... | collective-permute-start | bytes 3072008 | tf_op jit(solution)/shard_map/ppermute | solution.py:319
  65.0 1.6 collective-permute-start.20
  66.7 4.7 %collective-permute-done.20 = f32[5,2,16,256]{3,2,1,0:T(8,128)S(1)} collective-permute-done((f32[5,2,16,256]{3,2,1,0:T(8,128)S(1)}, f32[5,2,16,256]{3,2,1,0:T(8,128)S(1)}, u32[]{:S(2)}, u32[]{:S(2)}) %collective-permute-start.20) | collective-permute-done | bytes 163872 | tf_op jit(solution)/shard_map/ppermute | solution.py:238
  71.5 1.5 collective-permute-start.21
  73.1 1.4 collective-permute-start.15
  75.8 1.5 collective-permute-start.11
  77.2 8.6 %collective-permute-done.22 = bf16[256,2000]{0,1:T(8,128)(2,1)} collective-permute-done((bf16[256,2000]{0,1:T(8,128)(2,1)}, bf16[256,2000]{0,1:T(8,128)(2,1)}, u32[]{:S(2)}, u32[]{:S(2)}) %collective-permute-start.22) | collective-permute-done | bytes 1024032 | tf_op jit(solution)/shard_map/ppermute | solution.py:319
  87.2 1.5 collective-permute-start.17
  88.9 2.3 %copy.39.refs_1_ = bf16[256,2000]{1,0:T(8,128)(2,1)} copy(bf16[256,2000]{0,1:T(8,128)(2,1)} %collective-permute-done.22) | data formatting | bytes 2048000 | tf_op jit(solution)/shard_map/ppermute | solution.py:319
  91.2 10.7 %collective-permute-done.9.refs_2_.refs_5_ = bf16[2000,128]{1,0:T(8,128)(2,1)} collective-permute-done((bf16[2000,128]{1,0:T(8,128)(2,1)S(1)}, bf16[2000,128]{1,0:T(8,128)(2,1)}, u32[]{:S(2)}, u32[]{:S(2)}) %collective-permute-start.9) | collective-permute-done | bytes 512032 | tf_op jit(solution)/shard_map/ppermute | solution.py:319
  103.2 3.1 %project.3 = (f32[6,4,16,256]{3,2,1,0:T(8,128)S(1)}, f32[6,4,16,256]{3,2,1,0:T(8,128)S(1)}) custom-call(s32[1]{0:T(128)} %bitcast.2.core_ref, bf16[256,2000]{1,0:T(8,128)(2,1)S(1)} %maximum_select_fusion.refs_0_, bf16[256,2000]{1,0:T(8,128)(2,1)S(1)} %copy-done, bf16[2000,128]{1,0:T(8,128)(2,1)} %collective-permute-done.9.refs_2_.refs_5_, ...), custom_call_target="tpu_custom_call" | custom-call | flops 786432000 | bytes 4370432 | tf_op jit(solution)/shard_map/project/pallas_call | solution.py:143
  106.4 1.6 collective-permute-done.23
  108.2 1.6 collective-permute-start.24
  110.5 1.3 collective-permute-start.28
  112.5 1.3 collective-permute-start.26
  115.2 1.5 collective-permute-start.25
  116.8 3.1 %collective-permute-done.25 = f32[6,1,16,256]{3,2,1,0:T(8,128)S(1)} collective-permute-done((f32[6,1,16,256]{3,2,1,0:T(8,128)S(1)}, f32[6,1,16,256]{3,2,1,0:T(8,128)S(1)}, u32[]{:S(2)}, u32[]{:S(2)}) %collective-permute-start.25) | collective-permute-done | bytes 98336 | tf_op jit(solution)/shard_map/ppermute | solution.py:238
  120.2 18.0 %collective-permute-done.28.refs_12_ = bf16[2000,128]{1,0:T(8,128)(2,1)S(1)} collective-permute-done((bf16[2000,128]{1,0:T(8,128)(2,1)}, bf16[2000,128]{1,0:T(8,128)(2,1)S(1)}, u32[]{:S(2)}, u32[]{:S(2)}) %collective-permute-start.28) | collective-permute-done | bytes 512032 | tf_op jit(solution)/shard_map/ppermute | solution.py:319
  138.2 10.2 %collective-permute-done.26.refs_10_ = bf16[2000,128]{1,0:T(8,128)(2,1)S(1)} collective-permute-done((bf16[2000,128]{1,0:T(8,128)(2,1)}, bf16[2000,128]{1,0:T(8,128)(2,1)S(1)}, u32[]{:S(2)}, u32[]{:S(2)}) %collective-permute-start.26) | collective-permute-done | bytes 512032 | tf_op jit(solution)/shard_map/ppermute | solution.py:319
  148.6 3.5 %collective-permute-done.30 = f32[10,16]{1,0:T(8,128)S(1)} collective-permute-done((f32[10,16]{1,0:T(8,128)S(1)}, f32[10,16]{1,0:T(8,128)S(1)}, u32[]{:S(2)}, u32[]{:S(2)}) %collective-permute-start.30) | collective-permute-done | bytes 672 | tf_op jit(solution)/shard_map/ppermute | solution.py:238
  152.4 1.3 collective-permute-start.32
  153.7 2.9 %collective-permute-done.31 = f32[10,16]{1,0:T(8,128)S(1)} collective-permute-done((f32[10,16]{1,0:T(8,128)S(1)}, f32[10,16]{1,0:T(8,128)S(1)}, u32[]{:S(2)}, u32[]{:S(2)}) %collective-permute-start.31) | collective-permute-done | bytes 672 | tf_op jit(solution)/shard_map/ppermute | solution.py:238
  156.7 1.7 collective-permute-done.32
  158.5 1.6 collective-permute-start.33
  160.1 1.5 collective-permute-start.36
  163.2 4.0 %collective-permute-done.34 = bf16[11,2,16,128]{3,2,0,1:T(8,128)(2,1)S(1)} collective-permute-done((bf16[11,2,16,128]{3,2,0,1:T(8,128)(2,1)S(1)}, bf16[11,2,16,128]{3,2,0,1:T(8,128)(2,1)S(1)}, u32[]{:S(2)}, u32[]{:S(2)}) %collective-permute-start.34) | collective-permute-done | bytes 90144 | tf_op jit(solution)/shard_map/ppermute | solution.py:238
  167.4 1.4 collective-permute-done.35
  168.8 3.8 %collective-permute-done.36.refs_14_ = bf16[2000,128]{1,0:T(8,128)(2,1)} collective-permute-done((bf16[2000,128]{1,0:T(8,128)(2,1)}, bf16[2000,128]{1,0:T(8,128)(2,1)}, u32[]{:S(2)}, u32[]{:S(2)}) %collective-permute-start.36) | collective-permute-done | bytes 512032 | tf_op jit(solution)/shard_map/ppermute | solution.py:319
  172.6 5.2 %contract.1 = (f32[64,2000]{1,0:T(8,128)}, f32[64,2000]{1,0:T(8,128)}) custom-call(s32[1]{0:T(128)} %bitcast.2.core_ref, bf16[1408,128]{1,0:T(8,128)(2,1)S(1)} %bitcast.64, bf16[2000,128]{1,0:T(8,128)(2,1)S(1)} %add.312.refs_1_.refs_0_, bf16[2000,128]{1,0:T(8,128)(2,1)S(1)} %add.314.refs_2_.refs_1_, bf16[2000,128]{1,0:T(8,128)(2,1)S(1)} %add.313.refs_3_.refs_2_, ...), custom_call_target="tpu_custom_call" | custom-call | flops 720896000 | bytes 6656000 | tf_op jit(solution)/shard_map/contract/pallas_call | solution.py:186
  180.8 2.3 %conditional.1 = (f32[64,4000]{1,0:T(8,128)S(1)}) conditional(s32[]{:T(128)} %convert_element_type.31, (s32[8]{0:T(128)S(1)}, f32[256]{0:T(256)S(1)}, bf16[4000,64]{0,1:T(8,128)(2,1)}, bf16[4000,64]{0,1:T(8,128)(2,1)}, s32[8,32]{1,0:T(8,128)S(1)}, /*index=5*/bf16[256,4000]{0,1:T(8,128)(2,1)}) %tuple.122, (s32[]{:T(128)}, f32[64,2000]{1,0:T(8,128)}, ...), branch_computations={%region_10.18_spmd, %region_18.19_spmd} | conditional | flops 398105376 | bytes 73837632 | solution.py:423
  181.6 1.5 finish.1
  (137 shorter events, 20.6 us)
Async XLA Ops:
  0.0 3.1 %copy-start.11 = (s32[8,32]{1,0:T(8,128)S(1)}, s32[8,32]{1,0:T(8,128)}, u32[]{:S(2)}) copy-start(s32[8,32]{1,0:T(8,128)} %param.19) | copy-start | bytes 3076
  0.0 3.2 %copy-start.13 = (s32[8]{0:T(128)S(1)}, s32[8]{0:T(128)}, u32[]{:S(2)}) copy-start(s32[8]{0:T(128)} %param.18) | copy-start | bytes 100
  0.0 3.3 %copy-start.12 = (f32[256]{0:T(256)S(1)}, f32[256]{0:T(256)}, u32[]{:S(2)}) copy-start(f32[256]{0:T(256)} %param.17) | copy-start | bytes 3076
  2.7 14.1 %collective-permute-start.6 = (bf16[2000,256]{1,0:T(8,128)(2,1)}, bf16[2000,256]{1,0:T(8,128)(2,1)S(1)}, u32[]{:S(2)}, u32[]{:S(2)}) collective-permute-start(bf16[2000,256]{1,0:T(8,128)(2,1)} %get-tuple-element.442), channel_id=1, source_target_pairs={{0,4},{4,0},{8,12},{12,8},{16,20},{20,16},{24,28},{28,24},{1,5},{5... | collective-permute-start | bytes 3072008 | tf_op jit(solution)/shard_map/ppermute | solution.py:238
  3.2 12.3 %collective-permute-start.7 = (s32[16,8]{0,1:T(8,128)S(1)}, s32[16,8]{0,1:T(8,128)S(1)}, u32[]{:S(2)}, u32[]{:S(2)}) collective-permute-start(s32[16,8]{0,1:T(8,128)S(1)} %get-tuple-element.452), channel_id=1, source_target_pairs={{0,4},{4,0},{8,12},{12,8},{16,20},{20,16},{24,28},{28,24},{1,5},{5... | collective-permute-start | bytes 1544 | tf_op jit(solution)/shard_map/ppermute | solution.py:238
  3.3 2.6 %collective-permute-start.3 = (f32[1,264]{1,0:T(1,128)S(1)}, f32[1,264]{1,0:T(1,128)S(1)}, u32[]{:S(2)}, u32[]{:S(2)}) collective-permute-start(f32[1,264]{1,0:T(1,128)S(1)} %broadcast_in_dim.162), channel_id=1, source_target_pairs={{0,4},{4,0},{8,12},{12,8},{16,20},{20,16},{24,28},{28,24},{1,5},{5... | collective-permute-start | bytes 3176 | tf_op jit(solution)/shard_map/ppermute | solution.py:238
  6.0 4.3 %collective-permute-start.4 = (f32[2,264]{1,0:T(2,128)S(1)}, f32[2,264]{1,0:T(2,128)S(1)}, u32[]{:S(2)}, u32[]{:S(2)}) collective-permute-start(f32[2,264]{1,0:T(2,128)S(1)} %maximum_select_fusion.6), channel_id=1, source_target_pairs={{0,8},{4,12},{8,0},{12,4},{16,24},{20,28},{24,16},{28,20},{1,9},{5... | collective-permute-start | bytes 6344 | tf_op jit(solution)/shard_map/ppermute | solution.py:238
  10.1 19.1 %collective-permute-start.18 = (bf16[128,2000]{1,0:T(8,128)(2,1)}, bf16[128,2000]{1,0:T(8,128)(2,1)S(1)}, u32[]{:S(2)}, u32[]{:S(2)}) collective-permute-start(bf16[128,2000]{1,0:T(8,128)(2,1)} %get-tuple-element.445), channel_id=1, source_target_pairs={{0,4},{4,0},{8,12},{12,8},{16,20},{20,16},{24,28},{28,24},{1,5},{5... | collective-permute-start | bytes 1536008 | tf_op jit(solution)/shard_map/ppermute | solution.py:238
  10.3 5.4 %collective-permute-start.5 = (f32[4,264]{1,0:T(4,128)S(1)}, f32[4,264]{1,0:T(4,128)S(1)}, u32[]{:S(2)}, u32[]{:S(2)}) collective-permute-start(f32[4,264]{1,0:T(4,128)S(1)} %maximum_select_fusion.5), channel_id=1, source_target_pairs={{0,16},{4,20},{8,24},{12,28},{16,0},{20,4},{24,8},{28,12},{1,17},{... | collective-permute-start | bytes 12680 | tf_op jit(solution)/shard_map/ppermute | solution.py:238
  16.7 17.9 %copy-start.6 = (bf16[64,2000]{1,0:T(8,128)(2,1)S(1)}, bf16[64,2000]{1,0:T(8,128)(2,1)}, u32[]{:S(2)}) copy-start(bf16[64,2000]{1,0:T(8,128)(2,1)} %get-tuple-element.447) | copy-start | bytes 768004
  18.5 16.4 %collective-permute-start.14 = (bf16[2000,128]{1,0:T(8,128)(2,1)S(1)}, bf16[2000,128]{1,0:T(8,128)(2,1)S(1)}, u32[]{:S(2)}, u32[]{:S(2)}) collective-permute-start(bf16[2000,128]{1,0:T(8,128)(2,1)S(1)} %get-tuple-element.349), channel_id=1, source_target_pairs={{0,8},{4,12},{8,16},{12,20},{16,24},{20,28},{1,9},{5,13},{9,17},{1... | collective-permute-start | bytes 1536008 | tf_op jit(solution)/shard_map/ppermute | solution.py:319
  22.1 16.5 %collective-permute-start.12 = (bf16[2000,128]{1,0:T(8,128)(2,1)S(1)}, bf16[2000,128]{1,0:T(8,128)(2,1)S(1)}, u32[]{:S(2)}, u32[]{:S(2)}) collective-permute-start(bf16[2000,128]{1,0:T(8,128)(2,1)S(1)} %get-tuple-element.348), channel_id=1, source_target_pairs={{8,0},{12,4},{16,8},{20,12},{24,16},{28,20},{9,1},{13,5},{17,9},{2... | collective-permute-start | bytes 1536008 | tf_op jit(solution)/shard_map/ppermute | solution.py:319
  23.4 21.7 %collective-permute-start.10 = (bf16[2000,128]{1,0:T(8,128)(2,1)S(1)}, bf16[2000,128]{1,0:T(8,128)(2,1)S(1)}, u32[]{:S(2)}, u32[]{:S(2)}) collective-permute-start(bf16[2000,128]{1,0:T(8,128)(2,1)S(1)} %get-tuple-element.347), channel_id=1, source_target_pairs={{0,8},{4,12},{8,16},{12,20},{16,24},{20,28},{1,9},{5,13},{9,17},{1... | collective-permute-start | bytes 1536008 | tf_op jit(solution)/shard_map/ppermute | solution.py:319
  27.9 19.3 %collective-permute-start.8 = (bf16[2000,128]{1,0:T(8,128)(2,1)S(1)}, bf16[2000,128]{1,0:T(8,128)(2,1)S(1)}, u32[]{:S(2)}, u32[]{:S(2)}) collective-permute-start(bf16[2000,128]{1,0:T(8,128)(2,1)S(1)} %get-tuple-element.346), channel_id=1, source_target_pairs={{8,0},{12,4},{16,8},{20,12},{24,16},{28,20},{9,1},{13,5},{17,9},{2... | collective-permute-start | bytes 1536008 | tf_op jit(solution)/shard_map/ppermute | solution.py:319
  29.2 24.8 %collective-permute-start.16 = (bf16[2000,128]{1,0:T(8,128)(2,1)S(1)}, bf16[2000,128]{1,0:T(8,128)(2,1)}, u32[]{:S(2)}, u32[]{:S(2)}) collective-permute-start(bf16[2000,128]{1,0:T(8,128)(2,1)S(1)} %get-tuple-element.350), channel_id=1, source_target_pairs={{0,8},{4,12},{24,16},{28,20},{1,9},{5,13},{25,17},{29,21},{2,10},{... | collective-permute-start | bytes 1536008 | tf_op jit(solution)/shard_map/ppermute | solution.py:319
  56.9 7.1 %collective-permute-start.19 = (f32[5,4,16,256]{3,2,1,0:T(8,128)}, f32[5,4,16,256]{3,2,1,0:T(8,128)}, u32[]{:S(2)}, u32[]{:S(2)}) collective-permute-start(f32[5,4,16,256]{3,2,1,0:T(8,128)} %get-tuple-element.352), channel_id=1, source_target_pairs={{0,4},{4,0},{8,12},{12,8},{16,20},{20,16},{24,28},{28,24},{1,5},{5... | collective-permute-start | bytes 983048 | tf_op jit(solution)/shard_map/ppermute | solution.py:238
  58.5 27.4 %collective-permute-start.22 = (bf16[256,2000]{0,1:T(8,128)(2,1)}, bf16[256,2000]{0,1:T(8,128)(2,1)}, u32[]{:S(2)}, u32[]{:S(2)}) collective-permute-start(bf16[256,2000]{0,1:T(8,128)(2,1)} %copy.38), channel_id=1, source_target_pairs={{0,8},{4,12},{24,16},{28,20},{1,9},{5,13},{25,17},{29,21},{2,10},{... | collective-permute-start | bytes 3072008 | tf_op jit(solution)/shard_map/ppermute | solution.py:319
  65.0 6.4 %collective-permute-start.20 = (f32[5,2,16,256]{3,2,1,0:T(8,128)S(1)}, f32[5,2,16,256]{3,2,1,0:T(8,128)S(1)}, u32[]{:S(2)}, u32[]{:S(2)}) collective-permute-start(f32[5,2,16,256]{3,2,1,0:T(8,128)S(1)} %slice_select_fusion.1), channel_id=1, source_target_pairs={{0,2},{1,3},{2,0},{3,1},{4,6},{5,7},{6,4},{7,5},{8,10},{9,11},{10,... | collective-permute-start | bytes 491528 | tf_op jit(solution)/shard_map/ppermute | solution.py:238
  71.5 15.7 %collective-permute-start.21 = (f32[5,1,16,256]{3,2,1,0:T(8,128)S(1)}, f32[5,1,16,256]{3,2,1,0:T(8,128)S(1)}, u32[]{:S(2)}, u32[]{:S(2)}) collective-permute-start(f32[5,1,16,256]{3,2,1,0:T(8,128)S(1)} %slice_select_fusion.3), channel_id=1, source_target_pairs={{0,1},{1,0},{2,3},{3,2},{4,5},{5,4},{6,7},{7,6},{8,9},{9,8},{10,11... | collective-permute-start | bytes 245768 | tf_op jit(solution)/shard_map/ppermute | solution.py:238
  73.1 18.1 %collective-permute-start.15 = (bf16[2000,128]{1,0:T(8,128)(2,1)S(1)}, bf16[2000,128]{1,0:T(8,128)(2,1)}, u32[]{:S(2)}, u32[]{:S(2)}) collective-permute-start(bf16[2000,128]{1,0:T(8,128)(2,1)S(1)} %add.315.refs_4_.refs_3_), channel_id=1, source_target_pairs={{8,16},{12,20},{16,24},{20,28},{9,17},{13,21},{17,25},{21,29},{10,... | collective-permute-start | bytes 1536008 | tf_op jit(solution)/shard_map/ppermute | solution.py:319
  74.5 16.7 %collective-permute-start.13 = (bf16[2000,128]{1,0:T(8,128)(2,1)S(1)}, bf16[2000,128]{1,0:T(8,128)(2,1)}, u32[]{:S(2)}, u32[]{:S(2)}) collective-permute-start(bf16[2000,128]{1,0:T(8,128)(2,1)S(1)} %add.314.refs_2_.refs_1_), channel_id=1, source_target_pairs={{8,0},{12,4},{16,8},{20,12},{9,1},{13,5},{17,9},{21,13},{10,2},{14... | collective-permute-start | bytes 1536008 | tf_op jit(solution)/shard_map/ppermute | solution.py:319
  75.8 15.4 %collective-permute-start.11 = (bf16[2000,128]{1,0:T(8,128)(2,1)S(1)}, bf16[2000,128]{1,0:T(8,128)(2,1)}, u32[]{:S(2)}, u32[]{:S(2)}) collective-permute-start(bf16[2000,128]{1,0:T(8,128)(2,1)S(1)} %add.313.refs_3_.refs_2_), channel_id=1, source_target_pairs={{8,16},{12,20},{16,24},{20,28},{9,17},{13,21},{17,25},{21,29},{10,... | collective-permute-start | bytes 1536008 | tf_op jit(solution)/shard_map/ppermute | solution.py:319
  85.9 16.1 %collective-permute-start.9 = (bf16[2000,128]{1,0:T(8,128)(2,1)S(1)}, bf16[2000,128]{1,0:T(8,128)(2,1)}, u32[]{:S(2)}, u32[]{:S(2)}) collective-permute-start(bf16[2000,128]{1,0:T(8,128)(2,1)S(1)} %add.312.refs_1_.refs_0_), channel_id=1, source_target_pairs={{8,0},{12,4},{16,8},{20,12},{9,1},{13,5},{17,9},{21,13},{10,2},{14... | collective-permute-start | bytes 1536008 | tf_op jit(solution)/shard_map/ppermute | solution.py:319
  87.2 14.8 %collective-permute-start.17 = (bf16[2000,128]{1,0:T(8,128)(2,1)}, bf16[2000,128]{1,0:T(8,128)(2,1)}, u32[]{:S(2)}, u32[]{:S(2)}) collective-permute-start(bf16[2000,128]{1,0:T(8,128)(2,1)} %collective-permute-done.16.refs_5_.refs_4_), channel_id=1, source_target_pairs={{8,16},{12,20},{16,8},{20,12},{9,17},{13,21},{17,9},{21,13},{10,18... | collective-permute-start | bytes 1536008 | tf_op jit(solution)/shard_map/ppermute | solution.py:319
  102.0 1.2 copy-start
  106.3 1.8 collective-permute-start.23
  108.2 7.0 %collective-permute-start.24 = (f32[6,2,16,256]{3,2,1,0:T(8,128)S(1)}, f32[6,2,16,256]{3,2,1,0:T(8,128)S(1)}, u32[]{:S(2)}, u32[]{:S(2)}) collective-permute-start(f32[6,2,16,256]{3,2,1,0:T(8,128)S(1)} %slice_select_fusion), channel_id=1, source_target_pairs={{0,2},{1,3},{2,0},{3,1},{4,6},{5,7},{6,4},{7,5},{8,10},{9,11},{10,... | collective-permute-start | bytes 589832 | tf_op jit(solution)/shard_map/ppermute | solution.py:238
  109.8 10.4 %collective-permute-start.29 = (bf16[2000,128]{1,0:T(8,128)(2,1)}, bf16[2000,128]{1,0:T(8,128)(2,1)S(1)}, u32[]{:S(2)}, u32[]{:S(2)}) collective-permute-start(bf16[2000,128]{1,0:T(8,128)(2,1)} %collective-permute-done.15.refs_5_.refs_8_), channel_id=1, source_target_pairs={{16,24},{20,28},{17,25},{21,29},{18,26},{22,30},{19,27},{23,31}} | collective-permute-start | bytes 1536008 | tf_op jit(solution)/shard_map/ppermute | solution.py:319
  110.5 27.7 %collective-permute-start.28 = (bf16[2000,128]{1,0:T(8,128)(2,1)}, bf16[2000,128]{1,0:T(8,128)(2,1)S(1)}, u32[]{:S(2)}, u32[]{:S(2)}) collective-permute-start(bf16[2000,128]{1,0:T(8,128)(2,1)} %collective-permute-done.13.refs_4_.refs_7_), channel_id=1, source_target_pairs={{8,0},{12,4},{9,1},{13,5},{10,2},{14,6},{11,3},{15,7}} | collective-permute-start | bytes 1536008 | tf_op jit(solution)/shard_map/ppermute | solution.py:319
  111.8 26.4 %collective-permute-start.27 = (bf16[2000,128]{1,0:T(8,128)(2,1)}, bf16[2000,128]{1,0:T(8,128)(2,1)S(1)}, u32[]{:S(2)}, u32[]{:S(2)}) collective-permute-start(bf16[2000,128]{1,0:T(8,128)(2,1)} %collective-permute-done.11.refs_3_.refs_6_), channel_id=1, source_target_pairs={{16,24},{20,28},{17,25},{21,29},{18,26},{22,30},{19,27},{23,31}} | collective-permute-start | bytes 1536008 | tf_op jit(solution)/shard_map/ppermute | solution.py:319
  112.5 35.9 %collective-permute-start.26 = (bf16[2000,128]{1,0:T(8,128)(2,1)}, bf16[2000,128]{1,0:T(8,128)(2,1)S(1)}, u32[]{:S(2)}, u32[]{:S(2)}) collective-permute-start(bf16[2000,128]{1,0:T(8,128)(2,1)} %collective-permute-done.9.refs_2_.refs_5_), channel_id=1, source_target_pairs={{8,0},{12,4},{9,1},{13,5},{10,2},{14,6},{11,3},{15,7}} | collective-permute-start | bytes 1536008 | tf_op jit(solution)/shard_map/ppermute | solution.py:319
  115.2 4.7 %collective-permute-start.25 = (f32[6,1,16,256]{3,2,1,0:T(8,128)S(1)}, f32[6,1,16,256]{3,2,1,0:T(8,128)S(1)}, u32[]{:S(2)}, u32[]{:S(2)}) collective-permute-start(f32[6,1,16,256]{3,2,1,0:T(8,128)S(1)} %slice_select_fusion.2), channel_id=1, source_target_pairs={{0,1},{1,0},{2,3},{3,2},{4,5},{5,4},{6,7},{7,6},{8,9},{9,8},{10,11... | collective-permute-start | bytes 294920 | tf_op jit(solution)/shard_map/ppermute | solution.py:238
  120.2 52.4 %copy-start.8 = (bf16[2000,128]{1,0:T(8,128)(2,1)}, bf16[2000,128]{1,0:T(8,128)(2,1)S(1)}, u32[]{:S(2)}) copy-start(bf16[2000,128]{1,0:T(8,128)(2,1)S(1)} %collective-permute-done.29.refs_13_) | copy-start | bytes 1536004
  138.2 10.2 %copy-start.9 = (bf16[2000,128]{1,0:T(8,128)(2,1)}, bf16[2000,128]{1,0:T(8,128)(2,1)S(1)}, u32[]{:S(2)}) copy-start(bf16[2000,128]{1,0:T(8,128)(2,1)S(1)} %collective-permute-done.28.refs_12_) | copy-start | bytes 1536004
  138.2 10.2 %copy-start.10 = (bf16[2000,128]{1,0:T(8,128)(2,1)}, bf16[2000,128]{1,0:T(8,128)(2,1)S(1)}, u32[]{:S(2)}) copy-start(bf16[2000,128]{1,0:T(8,128)(2,1)S(1)} %collective-permute-done.27.refs_11_) | copy-start | bytes 1536004
  148.4 3.7 %collective-permute-start.30 = (f32[10,16]{1,0:T(8,128)S(1)}, f32[10,16]{1,0:T(8,128)S(1)}, u32[]{:S(2)}, u32[]{:S(2)}) collective-permute-start(f32[10,16]{1,0:T(8,128)S(1)} %add.322), channel_id=1, source_target_pairs={{0,8},{4,12},{8,0},{12,4},{16,24},{20,28},{24,16},{28,20},{1,9},{5... | collective-permute-start | bytes 1928 | tf_op jit(solution)/shard_map/ppermute | solution.py:238
  152.1 4.5 %collective-permute-start.31 = (f32[10,16]{1,0:T(8,128)S(1)}, f32[10,16]{1,0:T(8,128)S(1)}, u32[]{:S(2)}, u32[]{:S(2)}) collective-permute-start(f32[10,16]{1,0:T(8,128)S(1)} %add.323), channel_id=1, source_target_pairs={{0,16},{4,20},{8,24},{12,28},{16,0},{20,4},{24,8},{28,12},{1,17},{... | collective-permute-start | bytes 1928 | tf_op jit(solution)/shard_map/ppermute | solution.py:238
  152.4 6.0 %collective-permute-start.32 = (f32[3,16,256]{2,1,0:T(8,128)S(1)}, f32[3,16,256]{2,1,0:T(8,128)S(1)}, u32[]{:S(2)}, u32[]{:S(2)}) collective-permute-start(f32[3,16,256]{2,1,0:T(8,128)S(1)} %slice_bitcast_fusion), channel_id=1, source_target_pairs={{8,0},{12,4},{16,24},{20,28},{9,1},{13,5},{17,25},{21,29},{10,2},{... | collective-permute-start | bytes 147464 | tf_op jit(solution)/shard_map/ppermute | solution.py:319
  158.5 4.1 %collective-permute-start.33 = (bf16[11,1,16,128]{3,2,0,1:T(8,128)(2,1)S(1)}, bf16[11,1,16,128]{3,2,0,1:T(8,128)(2,1)S(1)}, u32[]{:S(2)}, u32[]{:S(2)}) collective-permute-start(bf16[11,1,16,128]{3,2,0,1:T(8,128)(2,1)S(1)} %fusion.9), channel_id=1, source_target_pairs={{0,1},{1,0},{2,3},{3,2},{4,5},{5,4},{6,7},{7,6},{8,9},{9,8},{10,11... | collective-permute-start | bytes 135176 | tf_op jit(solution)/shard_map/ppermute | solution.py:238
  160.1 12.5 %collective-permute-start.36 = (bf16[2000,128]{1,0:T(8,128)(2,1)}, bf16[2000,128]{1,0:T(8,128)(2,1)}, u32[]{:S(2)}, u32[]{:S(2)}) collective-permute-start(bf16[2000,128]{1,0:T(8,128)(2,1)} %collective-permute-done.17.refs_6_.refs_9_), channel_id=1, source_target_pairs={{8,0},{12,4},{16,24},{20,28},{9,1},{13,5},{17,25},{21,29},{10,2},{... | collective-permute-start | bytes 1536008 | tf_op jit(solution)/shard_map/ppermute | solution.py:319
  162.7 4.6 %collective-permute-start.34 = (bf16[11,2,16,128]{3,2,0,1:T(8,128)(2,1)S(1)}, bf16[11,2,16,128]{3,2,0,1:T(8,128)(2,1)S(1)}, u32[]{:S(2)}, u32[]{:S(2)}) collective-permute-start(bf16[11,2,16,128]{3,2,0,1:T(8,128)(2,1)S(1)} %maximum_select_fusion.3), channel_id=1, source_target_pairs={{0,2},{1,3},{2,0},{3,1},{4,6},{5,7},{6,4},{7,5},{8,10},{9,11},{10,... | collective-permute-start | bytes 270344 | tf_op jit(solution)/shard_map/ppermute | solution.py:238
  167.3 1.5 collective-permute-start.35
  177.8 3.0 %collective-permute-start.37 = (f32[64,2000]{1,0:T(8,128)}, f32[64,2000]{1,0:T(8,128)S(1)}, u32[]{:S(2)}, u32[]{:S(2)}) collective-permute-start(f32[64,2000]{1,0:T(8,128)} %get-tuple-element.369), channel_id=1, source_target_pairs={{0,4},{4,0},{8,12},{12,8},{16,20},{20,16},{24,28},{28,24},{1,5},{5... | collective-permute-start | bytes 1536008 | tf_op jit(solution)/shard_map/ppermute | solution.py:238
  180.8 0.8 copy-start.7
  183.1 1.0 copy-start.5
where the time goes:
time: 185 us; the launch traced here: 184 us
  waiting for transfers between devices  95.3 us (52%)
  starting transfers between devices  50.5 us (27%)
  local copies, waits for them, and re-layouts  16.8 us (9%)
  Pallas kernels  14.4 us (8%)
  other arithmetic  5.02 us (3%)
  between operations  2.03 us (1%)
    ppermute x17, waiting for transfers between devices, sent(): return [lax.ppermute(x, 'grid', along(pairs)) for x in tiles]  71.6 us
    ppermute x17, starting transfers between devices, sent(): return [lax.ppermute(x, 'grid', along(pairs)) for x in tiles]  35.1 us
    ppermute x18, waiting for transfers between devices, flip(): return lax.ppermute(x, axis, [(i, i ^ bit) for i in range(count)])  23.6 us
    ppermute x18, starting transfers between devices, flip(): return lax.ppermute(x, axis, [(i, i ^ bit) for i in range(count)])  15.4 us
    pallas_call x2, Pallas kernels, project(): pl.pallas_call(body, out_shape=(shape, shape), in_specs=[SCALARS] + [WHOL...  5.94 us
    pallas_call x1, Pallas kernels, contract(): pl.pallas_call(body, out_shape=(shape, shape), in_specs=[SCALARS] + [WHOL...  5.16 us
  transfers between devices with their start and end apart: 35, of which 19 were waited for; matrix products, arithmetic and copies ran while one was open for 9% of the time, Pallas kernels for 1%

commit v1 on v0

--- a/solution.py
+++ b/solution.py
@@ -332,7 +332,8 @@
         if t == 1:
             from_right = [x + y for x, y in zip(from_right, high)]
             from_left = [x + y for x, y in zip(from_left, low)]
-            (far_panels,) = sent([panels], ends)
+            far_panels, edge = lax.optimization_barrier((panels, edge))
+            (far_panels,) = sent([far_panels], ends)
         right = jnp.where((chip + t <= last) | (t == 1), (chip + t) * per_window, none)
         left = jnp.where((chip + 1 - t > 0) | (t == 1), (chip + 1 - t) * per_window, none)
         edge_at = jnp.where(
@@ -350,15 +351,17 @@
         (x, y) for x, y in zip(sent(leftward, homes[:1]), sent(rightward, homes[1:]))
     ]
 
-    def summed(panels, tiles):
+    def summed(panels, tiles, beside=()):
         keep, give = project(panels, tiles, tile, shares, core)
         value = keep + flip(give, "grid", 1)
         for bit in reversed(occ_bits):
+            if bit == 1:
+                value, beside = lax.optimization_barrier((value, beside))
             upper = (occ & bit) != 0
             low_part, high_part = value[:, :bit], value[:, bit:]
             got = flip(jnp.where(upper, low_part, high_part), "occ", bit)
             value = jnp.where(upper, high_part, low_part) + got
-        return value[:, 0]
+        return value[:, 0], beside
 
     def shared_density(value, at):
         product = jnp.sum(value[:, :, : 2 * columns] * value[:, :, 2 * columns :], axis=2)
@@ -370,19 +373,16 @@
     second_jobs = sum(stages[per_group:], [])
     first_at = jnp.stack([at for _, at in first_jobs])
     second_at = jnp.stack([at for _, at in second_jobs])
-    first_value = summed([panels], [w for w, _ in first_jobs])
+    first_value, _ = summed([panels], [w for w, _ in first_jobs])
     far_count = per_window + 1
-    second_tiles, first_value = lax.optimization_barrier(
-        ([w for w, _ in second_jobs], first_value)
-    )
-    value = summed([panels, far_panels], second_tiles)
+    second_tiles, late[:1] = lax.optimization_barrier(([w for w, _ in second_jobs], late[:1]))
+    value, late[1:] = summed([panels, far_panels], second_tiles, late[1:])
     far_value = value[-far_count:]
     second_value = value[: len(second_jobs)]
     density = shared_density(first_value, first_at) + shared_density(
         jnp.concatenate((second_value, far_value)),
         jnp.concatenate((second_at, second_at[-far_count:])),
     )
-    density, late = lax.optimization_barrier((density, late))
     for bit in grid_bits[1:]:
         density = density + flip(density, "grid", bit)
     density = density * (1.0 / math.sqrt(total))

time: 185 us -> 152 us (0.82)
  waiting for transfers between devices: 95.3 us -> 67.5 us
  local copies, waits for them, and re-layouts: 16.8 us -> 13.6 us
    ppermute x17, waiting for transfers between devices: 71.6 us -> 43 us  [sent(): return [lax.ppermute(x, 'grid', along(pairs)) for x in tiles]]
  transfers between devices with their start and end apart: 35 -> 35, of which waited for: 19 -> 16; matrix products, arithmetic and copies ran while one was open for 9% -> 8% of each run, Pallas kernels for 1% -> 4%
where the time goes in v1:
time: 152 us
  waiting for transfers between devices  67.5 us (44%)
  starting transfers between devices  50.3 us (33%)
  local copies, waits for them, and re-layouts  13.6 us (9%)
  Pallas kernels  13.4 us (9%)
  other arithmetic  4.92 us (3%)
  between operations  1.95 us (1%)
    ppermute x17, waiting for transfers between devices, sent(): return [lax.ppermute(x, 'grid', along(pairs)) for x in tiles]  43 us
    ppermute x17, starting transfers between devices, sent(): return [lax.ppermute(x, 'grid', along(pairs)) for x in tiles]  35.4 us
    ppermute x18, waiting for transfers between devices, flip(): return lax.ppermute(x, axis, [(i, i ^ bit) for i in range(count)])  24.5 us
    ppermute x18, starting transfers between devices, flip(): return lax.ppermute(x, axis, [(i, i ^ bit) for i in range(count)])  14.9 us
    pallas_call x1, Pallas kernels, contract(): pl.pallas_call(body, out_shape=(shape, shape), in_specs=[SCALARS] + [WHOL...  5.16 us
    pallas_call x2, Pallas kernels, project(): pl.pallas_call(body, out_shape=(shape, shape), in_specs=[SCALARS] + [WHOL...  4.97 us
  transfers between devices with their start and end apart: 35, of which 16 were waited for; matrix products, arithmetic and copies ran while one was open for 8% of the time, Pallas kernels for 4%

profile of v1, /device:TPU:0, one launch (start us, length us, event | category | flops | bytes accessed | tf_op | source)
XLA Modules:
  0.0 151.7 jit_solution(9572332749345608854)
XLA Ops:
  0.0 2.7 %dynamic-slice_bitcast_fusion = (bf16[2000,256]{1,0:T(8,128)(2,1)}, bf16[2000,256]{1,0:T(8,128)(2,1)S(1)}) fusion(bf16[256,4000]{0,1:T(8,128)(2,1)} %param.14, s32[]{:T(128)S(6)} %select_n.292, s32[]{:T(128)S(6)} %select_n.291), kind=kLoop, calls=%fused_computation.16 | loop fusion | bytes 4096008 | tf_op jit(solution)/shard_map/dynamic_slice | solution.py:253
  4.0 1.2 dynamic-slice_bitcast_fusion.3
  6.0 3.1 %collective-permute-start.4 = (f32[2,264]{1,0:T(2,128)S(1)}, f32[2,264]{1,0:T(2,128)S(1)}, u32[]{:S(2)}, u32[]{:S(2)}) collective-permute-start(f32[2,264]{1,0:T(2,128)S(1)} %maximum_select_fusion.6), channel_id=1, source_target_pairs={{0,8},{4,12},{8,0},{12,4},{16,24},{20,28},{24,16},{28,20},{1,9},{5... | collective-permute-start | bytes 6344 | tf_op jit(solution)/shard_map/ppermute | solution.py:238
  9.2 1.5 collective-permute-done.4
  10.7 3.1 %collective-permute-start.5 = (f32[4,264]{1,0:T(4,128)S(1)}, f32[4,264]{1,0:T(4,128)S(1)}, u32[]{:S(2)}, u32[]{:S(2)}) collective-permute-start(f32[4,264]{1,0:T(4,128)S(1)} %maximum_select_fusion.5), channel_id=1, source_target_pairs={{0,16},{4,20},{8,24},{12,28},{16,0},{20,4},{24,8},{28,12},{1,17},{... | collective-permute-start | bytes 12680 | tf_op jit(solution)/shard_map/ppermute | solution.py:238
  16.4 1.8 %compact.1 = (bf16[2000,128]{1,0:T(8,128)(2,1)S(1)}, bf16[2000,128]{1,0:T(8,128)(2,1)S(1)}, bf16[2000,128]{1,0:T(8,128)(2,1)S(1)}, bf16[2000,128]{1,0:T(8,128)(2,1)S(1)}, bf16[2000,128]{1,0:T(8,128)(2,1)S(1)}) custom-call(s32[1]{0:T(128)} %bitcast.13.first_ref, bf16[2000,256]{1,0:T(8,128)(2,1)S(1)} %get-tuple-element.445.mine_ref, ...), custom_call_target="tpu_custom_call" | custom-call | flops 1048576000 | bytes 4096000 | tf_op jit(solution)/shard_map/compact/pallas_call | solution.py:95
  18.2 3.8 %collective-permute-start.12 = (bf16[2000,128]{1,0:T(8,128)(2,1)S(1)}, bf16[2000,128]{1,0:T(8,128)(2,1)S(1)}, u32[]{:S(2)}, u32[]{:S(2)}) collective-permute-start(bf16[2000,128]{1,0:T(8,128)(2,1)S(1)} %get-tuple-element.350), channel_id=1, source_target_pairs={{0,8},{4,12},{8,16},{12,20},{16,24},{20,28},{1,9},{5,13},{9,17},{1... | collective-permute-start | bytes 1536008 | tf_op jit(solution)/shard_map/ppermute | solution.py:319
  22.0 1.3 collective-permute-start.10
  23.3 4.6 %collective-permute-start.11 = (bf16[2000,128]{1,0:T(8,128)(2,1)S(1)}, bf16[2000,128]{1,0:T(8,128)(2,1)S(1)}, u32[]{:S(2)}, u32[]{:S(2)}) collective-permute-start(bf16[2000,128]{1,0:T(8,128)(2,1)S(1)} %get-tuple-element.348), channel_id=1, source_target_pairs={{0,8},{4,12},{8,16},{12,20},{16,24},{20,28},{1,9},{5,13},{9,17},{1... | collective-permute-start | bytes 1536008 | tf_op jit(solution)/shard_map/ppermute | solution.py:319
  27.9 1.3 collective-permute-start.9
  29.2 4.6 %collective-permute-start.13 = (bf16[2000,128]{1,0:T(8,128)(2,1)S(1)}, bf16[2000,128]{1,0:T(8,128)(2,1)S(1)}, u32[]{:S(2)}, u32[]{:S(2)}) collective-permute-start(bf16[2000,128]{1,0:T(8,128)(2,1)S(1)} %get-tuple-element.351), channel_id=1, source_target_pairs={{0,8},{4,12},{24,16},{28,20},{1,9},{5,13},{25,17},{29,21},{2,10},{... | collective-permute-start | bytes 1536008 | tf_op jit(solution)/shard_map/ppermute | solution.py:319
  34.3 1.5 collective-permute-start.21
  35.7 9.3 %collective-permute-done.11 = bf16[2000,128]{1,0:T(8,128)(2,1)S(1)} collective-permute-done((bf16[2000,128]{1,0:T(8,128)(2,1)S(1)}, bf16[2000,128]{1,0:T(8,128)(2,1)S(1)}, u32[]{:S(2)}, u32[]{:S(2)}) %collective-permute-start.11) | collective-permute-done | bytes 512032 | tf_op jit(solution)/shard_map/ppermute | solution.py:319
  45.2 1.5 collective-permute-start.19
  46.8 1.3 collective-permute-start.18
  48.1 4.6 %collective-permute-done.13.refs_5_.refs_4_ = bf16[2000,128]{1,0:T(8,128)(2,1)S(1)} collective-permute-done((bf16[2000,128]{1,0:T(8,128)(2,1)S(1)}, bf16[2000,128]{1,0:T(8,128)(2,1)S(1)}, u32[]{:S(2)}, u32[]{:S(2)}) %collective-permute-start.13) | collective-permute-done | bytes 512032 | tf_op jit(solution)/shard_map/ppermute | solution.py:319
  52.9 1.8 %project.2 = (f32[5,4,16,256]{3,2,1,0:T(8,128)S(1)}, f32[5,4,16,256]{3,2,1,0:T(8,128)}) custom-call(s32[1]{0:T(128)} %bitcast.2.core_ref, bf16[256,2000]{1,0:T(8,128)(2,1)S(1)} %maximum_select_fusion.refs_0_, bf16[2000,128]{1,0:T(8,128)(2,1)S(1)} %add.312.refs_1_.refs_0_, bf16[2000,128]{1,0:T(8,128)(2,1)S(1)} %add.313.refs_2_.refs_1_, ...), custom_call_target="tpu_custom_call" | custom-call | flops 655360000 | bytes 4239360 | tf_op jit(solution)/shard_map/project/pallas_call | solution.py:143
  54.9 1.3 copy.38
  56.2 5.4 %collective-permute-start.17 = (bf16[256,2000]{0,1:T(8,128)(2,1)}, bf16[256,2000]{0,1:T(8,128)(2,1)}, u32[]{:S(2)}, u32[]{:S(2)}) collective-permute-start(bf16[256,2000]{0,1:T(8,128)(2,1)} %copy.38), channel_id=1, source_target_pairs={{0,8},{4,12},{24,16},{28,20},{1,9},{5,13},{25,17},{29,21},{2,10},{... | collective-permute-start | bytes 3072008 | tf_op jit(solution)/shard_map/ppermute | solution.py:319
  61.6 1.3 collective-permute-start.20
  63.1 1.4 collective-permute-start.22
  64.5 1.5 collective-permute-start.24
  66.0 1.3 collective-permute-start.23
  68.5 9.7 %collective-permute-done.20.refs_4_.refs_7_ = bf16[2000,128]{1,0:T(8,128)(2,1)} collective-permute-done((bf16[2000,128]{1,0:T(8,128)(2,1)S(1)}, bf16[2000,128]{1,0:T(8,128)(2,1)}, u32[]{:S(2)}, u32[]{:S(2)}) %collective-permute-start.20) | collective-permute-done | bytes 512032 | tf_op jit(solution)/shard_map/ppermute | solution.py:319
  78.1 1.5 %collective-permute-start.15 = (f32[5,2,16,256]{3,2,1,0:T(8,128)S(1)}, f32[5,2,16,256]{3,2,1,0:T(8,128)S(1)}, u32[]{:S(2)}, u32[]{:S(2)}) collective-permute-start(f32[5,2,16,256]{3,2,1,0:T(8,128)S(1)} %slice_select_fusion.1), channel_id=1, source_target_pairs={{0,2},{1,3},{2,0},{3,1},{4,6},{5,7},{6,4},{7,5},{8,10},{9,11},{10,... | collective-permute-start | bytes 491528 | tf_op jit(solution)/shard_map/ppermute | solution.py:238
  79.8 8.6 %collective-permute-done.23.refs_10_ = bf16[2000,128]{1,0:T(8,128)(2,1)} collective-permute-done((bf16[2000,128]{1,0:T(8,128)(2,1)}, bf16[2000,128]{1,0:T(8,128)(2,1)}, u32[]{:S(2)}, u32[]{:S(2)}) %collective-permute-start.23) | collective-permute-done | bytes 512032 | tf_op jit(solution)/shard_map/ppermute | solution.py:319
  88.4 2.3 %copy.39.refs_1_ = bf16[256,2000]{1,0:T(8,128)(2,1)} copy(bf16[256,2000]{0,1:T(8,128)(2,1)} %collective-permute-done.17) | data formatting | bytes 2048000 | tf_op jit(solution)/shard_map/ppermute | solution.py:319
  90.7 1.2 copy-done
  91.9 3.1 %project.3 = (f32[6,4,16,256]{3,2,1,0:T(8,128)S(1)}, f32[6,4,16,256]{3,2,1,0:T(8,128)S(1)}) custom-call(s32[1]{0:T(128)} %bitcast.2.core_ref, bf16[256,2000]{1,0:T(8,128)(2,1)S(1)} %maximum_select_fusion.refs_0_, bf16[256,2000]{1,0:T(8,128)(2,1)S(1)} %copy-done, bf16[2000,128]{1,0:T(8,128)(2,1)} %collective-permute-done.18.refs_2_.refs_5_, ...), custom_call_target="tpu_custom_call" | custom-call | flops 786432000 | bytes 4370432 | tf_op jit(solution)/shard_map/project/pallas_call | solution.py:143
  95.2 1.6 %collective-permute-start.16 = (f32[5,1,16,256]{3,2,1,0:T(8,128)S(1)}, f32[5,1,16,256]{3,2,1,0:T(8,128)S(1)}, u32[]{:S(2)}, u32[]{:S(2)}) collective-permute-start(f32[5,1,16,256]{3,2,1,0:T(8,128)S(1)} %slice_select_fusion.3), channel_id=1, source_target_pairs={{0,1},{1,0},{2,3},{3,2},{4,5},{5,4},{6,7},{7,6},{8,9},{9,8},{10,11... | collective-permute-start | bytes 245768 | tf_op jit(solution)/shard_map/ppermute | solution.py:238
  97.4 1.3 collective-permute-start.27
  98.9 1.6 %collective-permute-start.26 = (f32[6,2,16,256]{3,2,1,0:T(8,128)S(1)}, f32[6,2,16,256]{3,2,1,0:T(8,128)S(1)}, u32[]{:S(2)}, u32[]{:S(2)}) collective-permute-start(f32[6,2,16,256]{3,2,1,0:T(8,128)S(1)} %slice_select_fusion), channel_id=1, source_target_pairs={{0,2},{1,3},{2,0},{3,1},{4,6},{5,7},{6,4},{7,5},{8,10},{9,11},{10,... | collective-permute-start | bytes 589832 | tf_op jit(solution)/shard_map/ppermute | solution.py:238
  100.6 5.4 %collective-permute-done.26 = f32[6,2,16,256]{3,2,1,0:T(8,128)S(1)} collective-permute-done((f32[6,2,16,256]{3,2,1,0:T(8,128)S(1)}, f32[6,2,16,256]{3,2,1,0:T(8,128)S(1)}, u32[]{:S(2)}, u32[]{:S(2)}) %collective-permute-start.26) | collective-permute-done | bytes 196640 | tf_op jit(solution)/shard_map/ppermute | solution.py:238
  106.0 7.3 %collective-permute-done.27.refs_12_ = bf16[2000,128]{1,0:T(8,128)(2,1)S(1)} collective-permute-done((bf16[2000,128]{1,0:T(8,128)(2,1)}, bf16[2000,128]{1,0:T(8,128)(2,1)S(1)}, u32[]{:S(2)}, u32[]{:S(2)}) %collective-permute-start.27) | collective-permute-done | bytes 512032 | tf_op jit(solution)/shard_map/ppermute | solution.py:319
  114.0 4.0 %collective-permute-done.29 = f32[6,1,16,256]{3,2,1,0:T(8,128)S(1)} collective-permute-done((f32[6,1,16,256]{3,2,1,0:T(8,128)S(1)}, f32[6,1,16,256]{3,2,1,0:T(8,128)S(1)}, u32[]{:S(2)}, u32[]{:S(2)}) %collective-permute-start.29) | collective-permute-done | bytes 98336 | tf_op jit(solution)/shard_map/ppermute | solution.py:238
  118.5 3.5 %collective-permute-done.30 = f32[10,16]{1,0:T(8,128)S(1)} collective-permute-done((f32[10,16]{1,0:T(8,128)S(1)}, f32[10,16]{1,0:T(8,128)S(1)}, u32[]{:S(2)}, u32[]{:S(2)}) %collective-permute-start.30) | collective-permute-done | bytes 672 | tf_op jit(solution)/shard_map/ppermute | solution.py:238
  122.4 1.3 collective-permute-start.32
  123.7 2.9 %collective-permute-done.31 = f32[10,16]{1,0:T(8,128)S(1)} collective-permute-done((f32[10,16]{1,0:T(8,128)S(1)}, f32[10,16]{1,0:T(8,128)S(1)}, u32[]{:S(2)}, u32[]{:S(2)}) %collective-permute-start.31) | collective-permute-done | bytes 672 | tf_op jit(solution)/shard_map/ppermute | solution.py:238
  126.7 1.7 %collective-permute-done.32 = f32[3,16,256]{2,1,0:T(8,128)S(1)} collective-permute-done((f32[3,16,256]{2,1,0:T(8,128)S(1)}, f32[3,16,256]{2,1,0:T(8,128)S(1)}, u32[]{:S(2)}, u32[]{:S(2)}) %collective-permute-start.32) | collective-permute-done | bytes 49184 | tf_op jit(solution)/shard_map/ppermute | solution.py:319
  129.1 1.5 collective-permute-start.36
  130.5 2.0 %collective-permute-done.33 = bf16[11,1,16,128]{3,2,0,1:T(8,128)(2,1)S(1)} collective-permute-done((bf16[11,1,16,128]{3,2,0,1:T(8,128)(2,1)S(1)}, bf16[11,1,16,128]{3,2,0,1:T(8,128)(2,1)S(1)}, u32[]{:S(2)}, u32[]{:S(2)}) %collective-permute-start.33) | collective-permute-done | bytes 45088 | tf_op jit(solution)/shard_map/ppermute | solution.py:238
  132.6 1.6 %collective-permute-start.34 = (bf16[11,2,16,128]{3,2,0,1:T(8,128)(2,1)S(1)}, bf16[11,2,16,128]{3,2,0,1:T(8,128)(2,1)S(1)}, u32[]{:S(2)}, u32[]{:S(2)}) collective-permute-start(bf16[11,2,16,128]{3,2,0,1:T(8,128)(2,1)S(1)} %maximum_select_fusion.3), channel_id=1, source_target_pairs={{0,2},{1,3},{2,0},{3,1},{4,6},{5,7},{6,4},{7,5},{8,10},{9,11},{10,... | collective-permute-start | bytes 270344 | tf_op jit(solution)/shard_map/ppermute | solution.py:238
  134.2 3.0 %collective-permute-done.34 = bf16[11,2,16,128]{3,2,0,1:T(8,128)(2,1)S(1)} collective-permute-done((bf16[11,2,16,128]{3,2,0,1:T(8,128)(2,1)S(1)}, bf16[11,2,16,128]{3,2,0,1:T(8,128)(2,1)S(1)}, u32[]{:S(2)}, u32[]{:S(2)}) %collective-permute-start.34) | collective-permute-done | bytes 90144 | tf_op jit(solution)/shard_map/ppermute | solution.py:238
  137.3 1.4 collective-permute-done.35
  138.8 1.7 %collective-permute-done.36.refs_14_ = bf16[2000,128]{1,0:T(8,128)(2,1)} collective-permute-done((bf16[2000,128]{1,0:T(8,128)(2,1)}, bf16[2000,128]{1,0:T(8,128)(2,1)}, u32[]{:S(2)}, u32[]{:S(2)}) %collective-permute-start.36) | collective-permute-done | bytes 512032 | tf_op jit(solution)/shard_map/ppermute | solution.py:319
  140.5 5.2 %contract.1 = (f32[64,2000]{1,0:T(8,128)}, f32[64,2000]{1,0:T(8,128)}) custom-call(s32[1]{0:T(128)} %bitcast.2.core_ref, bf16[1408,128]{1,0:T(8,128)(2,1)S(1)} %bitcast.64, bf16[2000,128]{1,0:T(8,128)(2,1)S(1)} %add.312.refs_1_.refs_0_, bf16[2000,128]{1,0:T(8,128)(2,1)S(1)} %add.313.refs_2_.refs_1_, bf16[2000,128]{1,0:T(8,128)(2,1)S(1)} %add.314.refs_3_.refs_2_, ...), custom_call_target="tpu_custom_call" | custom-call | flops 720896000 | bytes 6656000 | tf_op jit(solution)/shard_map/contract/pallas_call | solution.py:186
  148.4 2.3 %conditional.1 = (f32[64,4000]{1,0:T(8,128)S(1)}) conditional(s32[]{:T(128)} %convert_element_type.31, (s32[8]{0:T(128)S(1)}, f32[256]{0:T(256)S(1)}, bf16[4000,64]{0,1:T(8,128)(2,1)}, bf16[4000,64]{0,1:T(8,128)(2,1)}, s32[8,32]{1,0:T(8,128)S(1)}, /*index=5*/bf16[256,4000]{0,1:T(8,128)(2,1)}) %tuple.124, (s32[]{:T(128)}, f32[64,2000]{1,0:T(8,128)}, ...), branch_computations={%region_10.18_spmd, %region_18.19_spmd} | conditional | flops 398105376 | bytes 73837632 | solution.py:423
  149.2 1.5 finish.1
  (147 shorter events, 13.7 us)
Async XLA Ops:
  0.0 3.2 %copy-start.16 = (s32[8,32]{1,0:T(8,128)S(1)}, s32[8,32]{1,0:T(8,128)}, u32[]{:S(2)}) copy-start(s32[8,32]{1,0:T(8,128)} %param.19) | copy-start | bytes 3076
  0.0 3.3 %copy-start.18 = (s32[8]{0:T(128)S(1)}, s32[8]{0:T(128)}, u32[]{:S(2)}) copy-start(s32[8]{0:T(128)} %param.18) | copy-start | bytes 100
  0.0 3.3 %copy-start.17 = (f32[256]{0:T(256)S(1)}, f32[256]{0:T(256)}, u32[]{:S(2)}) copy-start(f32[256]{0:T(256)} %param.17) | copy-start | bytes 3076
  0.0 3.9 %copy-start.9 = (bf16[4000,64]{0,1:T(8,128)(2,1)S(1)}, bf16[4000,64]{0,1:T(8,128)(2,1)}, u32[]{:S(2)}) copy-start(bf16[4000,64]{0,1:T(8,128)(2,1)} %param.15) | copy-start | bytes 1536004
  0.0 3.9 %copy-start.10 = (bf16[4000,64]{0,1:T(8,128)(2,1)S(1)}, bf16[4000,64]{0,1:T(8,128)(2,1)}, u32[]{:S(2)}) copy-start(bf16[4000,64]{0,1:T(8,128)(2,1)} %param.16) | copy-start | bytes 1536004
  2.7 13.6 %collective-permute-start.7 = (bf16[2000,256]{1,0:T(8,128)(2,1)}, bf16[2000,256]{1,0:T(8,128)(2,1)S(1)}, u32[]{:S(2)}, u32[]{:S(2)}) collective-permute-start(bf16[2000,256]{1,0:T(8,128)(2,1)} %get-tuple-element.444), channel_id=1, source_target_pairs={{0,4},{4,0},{8,12},{12,8},{16,20},{20,16},{24,28},{28,24},{1,5},{5... | collective-permute-start | bytes 3072008 | tf_op jit(solution)/shard_map/ppermute | solution.py:238
  3.3 11.1 %collective-permute-start.8 = (s32[16,8]{0,1:T(8,128)S(1)}, s32[16,8]{0,1:T(8,128)S(1)}, u32[]{:S(2)}, u32[]{:S(2)}) collective-permute-start(s32[16,8]{0,1:T(8,128)S(1)} %get-tuple-element.454), channel_id=1, source_target_pairs={{0,4},{4,0},{8,12},{12,8},{16,20},{20,16},{24,28},{28,24},{1,5},{5... | collective-permute-start | bytes 1544 | tf_op jit(solution)/shard_map/ppermute | solution.py:238
  3.4 2.6 %collective-permute-start.3 = (f32[1,264]{1,0:T(1,128)S(1)}, f32[1,264]{1,0:T(1,128)S(1)}, u32[]{:S(2)}, u32[]{:S(2)}) collective-permute-start(f32[1,264]{1,0:T(1,128)S(1)} %broadcast_in_dim.162), channel_id=1, source_target_pairs={{0,4},{4,0},{8,12},{12,8},{16,20},{20,16},{24,28},{28,24},{1,5},{5... | collective-permute-start | bytes 3176 | tf_op jit(solution)/shard_map/ppermute | solution.py:238
  5.2 24.0 %collective-permute-start.6 = (bf16[128,2000]{1,0:T(8,128)(2,1)}, bf16[128,2000]{1,0:T(8,128)(2,1)S(1)}, u32[]{:S(2)}, u32[]{:S(2)}) collective-permute-start(bf16[128,2000]{1,0:T(8,128)(2,1)} %get-tuple-element.447), channel_id=1, source_target_pairs={{0,4},{4,0},{8,12},{12,8},{16,20},{20,16},{24,28},{28,24},{1,5},{5... | collective-permute-start | bytes 1536008 | tf_op jit(solution)/shard_map/ppermute | solution.py:238
  6.0 4.7 %collective-permute-start.4 = (f32[2,264]{1,0:T(2,128)S(1)}, f32[2,264]{1,0:T(2,128)S(1)}, u32[]{:S(2)}, u32[]{:S(2)}) collective-permute-start(f32[2,264]{1,0:T(2,128)S(1)} %maximum_select_fusion.6), channel_id=1, source_target_pairs={{0,8},{4,12},{8,0},{12,4},{16,24},{20,28},{24,16},{28,20},{1,9},{5... | collective-permute-start | bytes 6344 | tf_op jit(solution)/shard_map/ppermute | solution.py:238
  10.7 4.7 %collective-permute-start.5 = (f32[4,264]{1,0:T(4,128)S(1)}, f32[4,264]{1,0:T(4,128)S(1)}, u32[]{:S(2)}, u32[]{:S(2)}) collective-permute-start(f32[4,264]{1,0:T(4,128)S(1)} %maximum_select_fusion.5), channel_id=1, source_target_pairs={{0,16},{4,20},{8,24},{12,28},{16,0},{20,4},{24,8},{28,12},{1,17},{... | collective-permute-start | bytes 12680 | tf_op jit(solution)/shard_map/ppermute | solution.py:238
  16.4 17.5 %copy-start.12 = (bf16[64,2000]{1,0:T(8,128)(2,1)S(1)}, bf16[64,2000]{1,0:T(8,128)(2,1)}, u32[]{:S(2)}) copy-start(bf16[64,2000]{1,0:T(8,128)(2,1)} %get-tuple-element.449) | copy-start | bytes 768004
  18.2 15.9 %collective-permute-start.12 = (bf16[2000,128]{1,0:T(8,128)(2,1)S(1)}, bf16[2000,128]{1,0:T(8,128)(2,1)S(1)}, u32[]{:S(2)}, u32[]{:S(2)}) collective-permute-start(bf16[2000,128]{1,0:T(8,128)(2,1)S(1)} %get-tuple-element.350), channel_id=1, source_target_pairs={{0,8},{4,12},{8,16},{12,20},{16,24},{20,28},{1,9},{5,13},{9,17},{1... | collective-permute-start | bytes 1536008 | tf_op jit(solution)/shard_map/ppermute | solution.py:319
  22.0 30.7 %collective-permute-start.10 = (bf16[2000,128]{1,0:T(8,128)(2,1)S(1)}, bf16[2000,128]{1,0:T(8,128)(2,1)S(1)}, u32[]{:S(2)}, u32[]{:S(2)}) collective-permute-start(bf16[2000,128]{1,0:T(8,128)(2,1)S(1)} %get-tuple-element.349), channel_id=1, source_target_pairs={{8,0},{12,4},{16,8},{20,12},{24,16},{28,20},{9,1},{13,5},{17,9},{2... | collective-permute-start | bytes 1536008 | tf_op jit(solution)/shard_map/ppermute | solution.py:319
  23.3 21.7 %collective-permute-start.11 = (bf16[2000,128]{1,0:T(8,128)(2,1)S(1)}, bf16[2000,128]{1,0:T(8,128)(2,1)S(1)}, u32[]{:S(2)}, u32[]{:S(2)}) collective-permute-start(bf16[2000,128]{1,0:T(8,128)(2,1)S(1)} %get-tuple-element.348), channel_id=1, source_target_pairs={{0,8},{4,12},{8,16},{12,20},{16,24},{20,28},{1,9},{5,13},{9,17},{1... | collective-permute-start | bytes 1536008 | tf_op jit(solution)/shard_map/ppermute | solution.py:319
  27.9 18.7 %collective-permute-start.9 = (bf16[2000,128]{1,0:T(8,128)(2,1)S(1)}, bf16[2000,128]{1,0:T(8,128)(2,1)S(1)}, u32[]{:S(2)}, u32[]{:S(2)}) collective-permute-start(bf16[2000,128]{1,0:T(8,128)(2,1)S(1)} %get-tuple-element.347), channel_id=1, source_target_pairs={{8,0},{12,4},{16,8},{20,12},{24,16},{28,20},{9,1},{13,5},{17,9},{2... | collective-permute-start | bytes 1536008 | tf_op jit(solution)/shard_map/ppermute | solution.py:319
  29.2 23.5 %collective-permute-start.13 = (bf16[2000,128]{1,0:T(8,128)(2,1)S(1)}, bf16[2000,128]{1,0:T(8,128)(2,1)S(1)}, u32[]{:S(2)}, u32[]{:S(2)}) collective-permute-start(bf16[2000,128]{1,0:T(8,128)(2,1)S(1)} %get-tuple-element.351), channel_id=1, source_target_pairs={{0,8},{4,12},{24,16},{28,20},{1,9},{5,13},{25,17},{29,21},{2,10},{... | collective-permute-start | bytes 1536008 | tf_op jit(solution)/shard_map/ppermute | solution.py:319
  34.3 28.8 %collective-permute-start.21 = (bf16[2000,128]{1,0:T(8,128)(2,1)S(1)}, bf16[2000,128]{1,0:T(8,128)(2,1)}, u32[]{:S(2)}, u32[]{:S(2)}) collective-permute-start(bf16[2000,128]{1,0:T(8,128)(2,1)S(1)} %add.315.refs_4_.refs_3_), channel_id=1, source_target_pairs={{8,16},{12,20},{16,24},{20,28},{9,17},{13,21},{17,25},{21,29},{10,... | collective-permute-start | bytes 1536008 | tf_op jit(solution)/shard_map/ppermute | solution.py:319
  45.2 19.3 %collective-permute-start.19 = (bf16[2000,128]{1,0:T(8,128)(2,1)S(1)}, bf16[2000,128]{1,0:T(8,128)(2,1)}, u32[]{:S(2)}, u32[]{:S(2)}) collective-permute-start(bf16[2000,128]{1,0:T(8,128)(2,1)S(1)} %add.314.refs_3_.refs_2_), channel_id=1, source_target_pairs={{8,16},{12,20},{16,24},{20,28},{9,17},{13,21},{17,25},{21,29},{10,... | collective-permute-start | bytes 1536008 | tf_op jit(solution)/shard_map/ppermute | solution.py:319
  46.8 19.2 %collective-permute-start.18 = (bf16[2000,128]{1,0:T(8,128)(2,1)S(1)}, bf16[2000,128]{1,0:T(8,128)(2,1)}, u32[]{:S(2)}, u32[]{:S(2)}) collective-permute-start(bf16[2000,128]{1,0:T(8,128)(2,1)S(1)} %add.312.refs_1_.refs_0_), channel_id=1, source_target_pairs={{8,0},{12,4},{16,8},{20,12},{9,1},{13,5},{17,9},{21,13},{10,2},{14... | collective-permute-start | bytes 1536008 | tf_op jit(solution)/shard_map/ppermute | solution.py:319
  52.8 2.0 %copy-start.1 = (bf16[2000,128]{1,0:T(8,128)(2,1)}, bf16[2000,128]{1,0:T(8,128)(2,1)S(1)}, u32[]{:S(2)}) copy-start(bf16[2000,128]{1,0:T(8,128)(2,1)S(1)} %collective-permute-done.13.refs_5_.refs_4_) | copy-start | bytes 1536004
  54.7 6.9 %collective-permute-start.14 = (f32[5,4,16,256]{3,2,1,0:T(8,128)}, f32[5,4,16,256]{3,2,1,0:T(8,128)}, u32[]{:S(2)}, u32[]{:S(2)}) collective-permute-start(f32[5,4,16,256]{3,2,1,0:T(8,128)} %get-tuple-element.354), channel_id=1, source_target_pairs={{0,4},{4,0},{8,12},{12,8},{16,20},{20,16},{24,28},{28,24},{1,5},{5... | collective-permute-start | bytes 983048 | tf_op jit(solution)/shard_map/ppermute | solution.py:238
  56.2 32.2 %collective-permute-start.17 = (bf16[256,2000]{0,1:T(8,128)(2,1)}, bf16[256,2000]{0,1:T(8,128)(2,1)}, u32[]{:S(2)}, u32[]{:S(2)}) collective-permute-start(bf16[256,2000]{0,1:T(8,128)(2,1)} %copy.38), channel_id=1, source_target_pairs={{0,8},{4,12},{24,16},{28,20},{1,9},{5,13},{25,17},{29,21},{2,10},{... | collective-permute-start | bytes 3072008 | tf_op jit(solution)/shard_map/ppermute | solution.py:319
  61.6 16.5 %collective-permute-start.20 = (bf16[2000,128]{1,0:T(8,128)(2,1)S(1)}, bf16[2000,128]{1,0:T(8,128)(2,1)}, u32[]{:S(2)}, u32[]{:S(2)}) collective-permute-start(bf16[2000,128]{1,0:T(8,128)(2,1)S(1)} %add.313.refs_2_.refs_1_), channel_id=1, source_target_pairs={{8,0},{12,4},{16,8},{20,12},{9,1},{13,5},{17,9},{21,13},{10,2},{14... | collective-permute-start | bytes 1536008 | tf_op jit(solution)/shard_map/ppermute | solution.py:319
  63.1 16.7 %collective-permute-start.22 = (bf16[2000,128]{1,0:T(8,128)(2,1)}, bf16[2000,128]{1,0:T(8,128)(2,1)}, u32[]{:S(2)}, u32[]{:S(2)}) collective-permute-start(bf16[2000,128]{1,0:T(8,128)(2,1)} %copy-done.1), channel_id=1, source_target_pairs={{8,16},{12,20},{16,8},{20,12},{9,17},{13,21},{17,9},{21,13},{10,18... | collective-permute-start | bytes 1536008 | tf_op jit(solution)/shard_map/ppermute | solution.py:319
  64.5 15.3 %collective-permute-start.24 = (bf16[2000,128]{1,0:T(8,128)(2,1)}, bf16[2000,128]{1,0:T(8,128)(2,1)}, u32[]{:S(2)}, u32[]{:S(2)}) collective-permute-start(bf16[2000,128]{1,0:T(8,128)(2,1)} %collective-permute-done.19.refs_3_.refs_6_), channel_id=1, source_target_pairs={{16,24},{20,28},{17,25},{21,29},{18,26},{22,30},{19,27},{23,31}} | collective-permute-start | bytes 1536008 | tf_op jit(solution)/shard_map/ppermute | solution.py:319
  66.0 22.4 %collective-permute-start.23 = (bf16[2000,128]{1,0:T(8,128)(2,1)}, bf16[2000,128]{1,0:T(8,128)(2,1)}, u32[]{:S(2)}, u32[]{:S(2)}) collective-permute-start(bf16[2000,128]{1,0:T(8,128)(2,1)} %collective-permute-done.18.refs_2_.refs_5_), channel_id=1, source_target_pairs={{8,0},{12,4},{9,1},{13,5},{10,2},{14,6},{11,3},{15,7}} | collective-permute-start | bytes 1536008 | tf_op jit(solution)/shard_map/ppermute | solution.py:319
  68.4 9.7 %copy-start.7 = (f32[5,4,16,256]{3,2,1,0:T(8,128)}, f32[5,4,16,256]{3,2,1,0:T(8,128)S(1)}, u32[]{:S(2)}) copy-start(f32[5,4,16,256]{3,2,1,0:T(8,128)S(1)} %add.316) | copy-start | bytes 983044
  78.1 17.0 %collective-permute-start.15 = (f32[5,2,16,256]{3,2,1,0:T(8,128)S(1)}, f32[5,2,16,256]{3,2,1,0:T(8,128)S(1)}, u32[]{:S(2)}, u32[]{:S(2)}) collective-permute-start(f32[5,2,16,256]{3,2,1,0:T(8,128)S(1)} %slice_select_fusion.1), channel_id=1, source_target_pairs={{0,2},{1,3},{2,0},{3,1},{4,6},{5,7},{6,4},{7,5},{8,10},{9,11},{10,... | collective-permute-start | bytes 491528 | tf_op jit(solution)/shard_map/ppermute | solution.py:238
  90.7 1.2 copy-start
  91.9 3.2 %copy-start.8 = (f32[5,4,16,256]{3,2,1,0:T(8,128)S(1)}, f32[5,4,16,256]{3,2,1,0:T(8,128)}, u32[]{:S(2)}) copy-start(f32[5,4,16,256]{3,2,1,0:T(8,128)} %copy-done.7) | copy-start | bytes 983044
  95.0 3.7 %collective-permute-start.25 = (f32[6,4,16,256]{3,2,1,0:T(8,128)S(1)}, f32[6,4,16,256]{3,2,1,0:T(8,128)S(1)}, u32[]{:S(2)}, u32[]{:S(2)}) collective-permute-start(f32[6,4,16,256]{3,2,1,0:T(8,128)S(1)} %get-tuple-element.362), channel_id=1, source_target_pairs={{0,4},{4,0},{8,12},{12,8},{16,20},{20,16},{24,28},{28,24},{1,5},{5... | collective-permute-start | bytes 1179656 | tf_op jit(solution)/shard_map/ppermute | solution.py:238
  95.2 5.2 %collective-permute-start.16 = (f32[5,1,16,256]{3,2,1,0:T(8,128)S(1)}, f32[5,1,16,256]{3,2,1,0:T(8,128)S(1)}, u32[]{:S(2)}, u32[]{:S(2)}) collective-permute-start(f32[5,1,16,256]{3,2,1,0:T(8,128)S(1)} %slice_select_fusion.3), channel_id=1, source_target_pairs={{0,1},{1,0},{2,3},{3,2},{4,5},{5,4},{6,7},{7,6},{8,9},{9,8},{10,11... | collective-permute-start | bytes 245768 | tf_op jit(solution)/shard_map/ppermute | solution.py:238
  96.8 9.2 %collective-permute-start.28 = (bf16[2000,128]{1,0:T(8,128)(2,1)}, bf16[2000,128]{1,0:T(8,128)(2,1)S(1)}, u32[]{:S(2)}, u32[]{:S(2)}) collective-permute-start(bf16[2000,128]{1,0:T(8,128)(2,1)} %collective-permute-done.21.refs_5_.refs_8_), channel_id=1, source_target_pairs={{16,24},{20,28},{17,25},{21,29},{18,26},{22,30},{19,27},{23,31}} | collective-permute-start | bytes 1536008 | tf_op jit(solution)/shard_map/ppermute | solution.py:319
  97.4 15.9 %collective-permute-start.27 = (bf16[2000,128]{1,0:T(8,128)(2,1)}, bf16[2000,128]{1,0:T(8,128)(2,1)S(1)}, u32[]{:S(2)}, u32[]{:S(2)}) collective-permute-start(bf16[2000,128]{1,0:T(8,128)(2,1)} %collective-permute-done.20.refs_4_.refs_7_), channel_id=1, source_target_pairs={{8,0},{12,4},{9,1},{13,5},{10,2},{14,6},{11,3},{15,7}} | collective-permute-start | bytes 1536008 | tf_op jit(solution)/shard_map/ppermute | solution.py:319
  98.9 7.1 %collective-permute-start.26 = (f32[6,2,16,256]{3,2,1,0:T(8,128)S(1)}, f32[6,2,16,256]{3,2,1,0:T(8,128)S(1)}, u32[]{:S(2)}, u32[]{:S(2)}) collective-permute-start(f32[6,2,16,256]{3,2,1,0:T(8,128)S(1)} %slice_select_fusion), channel_id=1, source_target_pairs={{0,2},{1,3},{2,0},{3,1},{4,6},{5,7},{6,4},{7,5},{8,10},{9,11},{10,... | collective-permute-start | bytes 589832 | tf_op jit(solution)/shard_map/ppermute | solution.py:238
  106.0 34.5 %copy-start.2 = (bf16[2000,128]{1,0:T(8,128)(2,1)S(1)}, bf16[2000,128]{1,0:T(8,128)(2,1)}, u32[]{:S(2)}) copy-start(bf16[2000,128]{1,0:T(8,128)(2,1)} %copy-done.1) | copy-start | bytes 1536004
  106.0 34.5 %copy-start.14 = (bf16[2000,128]{1,0:T(8,128)(2,1)}, bf16[2000,128]{1,0:T(8,128)(2,1)S(1)}, u32[]{:S(2)}) copy-start(bf16[2000,128]{1,0:T(8,128)(2,1)S(1)} %collective-permute-done.28.refs_13_) | copy-start | bytes 1536004
  113.3 4.7 %copy-start.15 = (bf16[2000,128]{1,0:T(8,128)(2,1)}, bf16[2000,128]{1,0:T(8,128)(2,1)S(1)}, u32[]{:S(2)}) copy-start(bf16[2000,128]{1,0:T(8,128)(2,1)S(1)} %collective-permute-done.27.refs_12_) | copy-start | bytes 1536004
  113.3 4.7 %collective-permute-start.29 = (f32[6,1,16,256]{3,2,1,0:T(8,128)S(1)}, f32[6,1,16,256]{3,2,1,0:T(8,128)S(1)}, u32[]{:S(2)}, u32[]{:S(2)}) collective-permute-start(f32[6,1,16,256]{3,2,1,0:T(8,128)S(1)} %slice_select_fusion.2), channel_id=1, source_target_pairs={{0,1},{1,0},{2,3},{3,2},{4,5},{5,4},{6,7},{7,6},{8,9},{9,8},{10,11... | collective-permute-start | bytes 294920 | tf_op jit(solution)/shard_map/ppermute | solution.py:238
  118.3 3.7 %collective-permute-start.30 = (f32[10,16]{1,0:T(8,128)S(1)}, f32[10,16]{1,0:T(8,128)S(1)}, u32[]{:S(2)}, u32[]{:S(2)}) collective-permute-start(f32[10,16]{1,0:T(8,128)S(1)} %add.322), channel_id=1, source_target_pairs={{0,8},{4,12},{8,0},{12,4},{16,24},{20,28},{24,16},{28,20},{1,9},{5... | collective-permute-start | bytes 1928 | tf_op jit(solution)/shard_map/ppermute | solution.py:238
  122.0 4.5 %collective-permute-start.31 = (f32[10,16]{1,0:T(8,128)S(1)}, f32[10,16]{1,0:T(8,128)S(1)}, u32[]{:S(2)}, u32[]{:S(2)}) collective-permute-start(f32[10,16]{1,0:T(8,128)S(1)} %add.323), channel_id=1, source_target_pairs={{0,16},{4,20},{8,24},{12,28},{16,0},{20,4},{24,8},{28,12},{1,17},{... | collective-permute-start | bytes 1928 | tf_op jit(solution)/shard_map/ppermute | solution.py:238
  122.4 6.0 %collective-permute-start.32 = (f32[3,16,256]{2,1,0:T(8,128)S(1)}, f32[3,16,256]{2,1,0:T(8,128)S(1)}, u32[]{:S(2)}, u32[]{:S(2)}) collective-permute-start(f32[3,16,256]{2,1,0:T(8,128)S(1)} %slice_bitcast_fusion), channel_id=1, source_target_pairs={{8,0},{12,4},{16,24},{20,28},{9,1},{13,5},{17,25},{21,29},{10,2},{... | collective-permute-start | bytes 147464 | tf_op jit(solution)/shard_map/ppermute | solution.py:319
  128.5 4.1 %collective-permute-start.33 = (bf16[11,1,16,128]{3,2,0,1:T(8,128)(2,1)S(1)}, bf16[11,1,16,128]{3,2,0,1:T(8,128)(2,1)S(1)}, u32[]{:S(2)}, u32[]{:S(2)}) collective-permute-start(bf16[11,1,16,128]{3,2,0,1:T(8,128)(2,1)S(1)} %fusion.9), channel_id=1, source_target_pairs={{0,1},{1,0},{2,3},{3,2},{4,5},{5,4},{6,7},{7,6},{8,9},{9,8},{10,11... | collective-permute-start | bytes 135176 | tf_op jit(solution)/shard_map/ppermute | solution.py:238
  129.1 11.4 %collective-permute-start.36 = (bf16[2000,128]{1,0:T(8,128)(2,1)}, bf16[2000,128]{1,0:T(8,128)(2,1)}, u32[]{:S(2)}, u32[]{:S(2)}) collective-permute-start(bf16[2000,128]{1,0:T(8,128)(2,1)} %collective-permute-done.22.refs_6_.refs_9_), channel_id=1, source_target_pairs={{8,0},{12,4},{16,24},{20,28},{9,1},{13,5},{17,25},{21,29},{10,2},{... | collective-permute-start | bytes 1536008 | tf_op jit(solution)/shard_map/ppermute | solution.py:319
  132.6 4.6 %collective-permute-start.34 = (bf16[11,2,16,128]{3,2,0,1:T(8,128)(2,1)S(1)}, bf16[11,2,16,128]{3,2,0,1:T(8,128)(2,1)S(1)}, u32[]{:S(2)}, u32[]{:S(2)}) collective-permute-start(bf16[11,2,16,128]{3,2,0,1:T(8,128)(2,1)S(1)} %maximum_select_fusion.3), channel_id=1, source_target_pairs={{0,2},{1,3},{2,0},{3,1},{4,6},{5,7},{6,4},{7,5},{8,10},{9,11},{10,... | collective-permute-start | bytes 270344 | tf_op jit(solution)/shard_map/ppermute | solution.py:238
  137.2 1.5 collective-permute-start.35
  145.7 2.8 %collective-permute-start.37 = (f32[64,2000]{1,0:T(8,128)}, f32[64,2000]{1,0:T(8,128)S(1)}, u32[]{:S(2)}, u32[]{:S(2)}) collective-permute-start(f32[64,2000]{1,0:T(8,128)} %get-tuple-element.371), channel_id=1, source_target_pairs={{0,4},{4,0},{8,12},{12,8},{16,20},{20,16},{24,28},{28,24},{1,5},{5... | collective-permute-start | bytes 1536008 | tf_op jit(solution)/shard_map/ppermute | solution.py:238
  (2 other events, 1.8 us)
